TPU v7x, 128 devices: a whole 4x4x4 slice. The times are simulated.
128 devices in a mesh: bucket: 32 (over z, y, core), dom: 4 (over x).
Axes of the slice: x: 4, y: 4, z: 4, core: 2. Of those that a mesh axis runs over, the one named last changes fastest.
Arguments:
- left_table: float32 [262144, 128], P(('bucket', 'dom')), may hold values from -1.8 to 1.8
- right_table: float32 [262144, 128], P(('bucket', 'dom')), may hold values from -1.8 to 1.8
- left_state: float32 [262144], P(('bucket', 'dom')), may hold values from 0.01 to 1
- right_state: float32 [262144], P(('bucket', 'dom')), may hold values from 0.01 to 1
- sources: int32 [2097152], P(('bucket', 'dom')), may hold values from 0 to 8191
- targets: int32 [2097152], P(('bucket', 'dom')), may hold values from 0 to 8191
- relation_ids: int32 [2097152], P(('bucket', 'dom')), may hold values from 0 to 8191
- negatives: int32 [4096, 1024], P(('bucket', 'dom')), may hold values from 0 to 8191
- rotation: int32 [1], replicated, may hold values from 0 to 31
- relations: float32 [8192, 128], replicated, may hold values from -4 to 4
- relation_state: float32 [8192], replicated, may hold values from 0.01 to 1
Outputs:
- left_updated: float32 [262144, 128], P(('bucket', 'dom'))
- right_updated: float32 [262144, 128], P(('bucket', 'dom'))
- left_accum: float32 [262144], P(('bucket', 'dom'))
- right_accum: float32 [262144], P(('bucket', 'dom'))
- relations_updated: float32 [8192, 128], replicated
- relation_accum: float32 [8192], replicated
Inputs may be any that keep to these rules, and one draw needn't show every extreme that they name: Trainer b pairs left partition b with right partition (b + rotation) mod 32.
All inputs are finite; a program needn't handle non-finite values.
Results may differ from a plain program's by a relative error of at most 0.00012.
Values sent between devices are 32-bit elements; how exact they have to be, the bound alone decides.
A program may use at most 128 MiB of HBM per device.

v0:
```python
import jax
import jax.numpy as jnp
from jax import lax
from jax.sharding import PartitionSpec as P

learn_rate = 0.2
margin_gap = 1.0


def shifted(array, axis, by):
    size = lax.axis_size(axis)
    return lax.ppermute(array, axis, [(i, (i + by) % size) for i in range(size)])


def adagrad(param, state, grad):
    new_state = state + jnp.mean(grad * grad, axis=-1)
    return (param - learn_rate * grad / jnp.sqrt(new_state)[:, None], new_state)


def move_rows(tables, amount):
    trainers = lax.axis_size("bucket")
    for position in range(max(trainers - 1, 1).bit_length()):
        arrived = shifted((tables[0], tables[1]), "bucket", -(1 << position))
        chosen = amount >> position & 1 == 1
        tables = (
            jnp.where(chosen, arrived[0], tables[0]),
            jnp.where(chosen, arrived[1], tables[1]),
        )
    return tables


def body(
    left_table,
    right_table,
    left_state,
    right_state,
    sources,
    targets,
    relation_ids,
    negatives,
    rotation,
    relations,
    relation_state,
):
    high = lax.Precision.HIGHEST
    trainers = lax.axis_size("bucket")
    forward = jnp.mod(rotation[0], trainers)
    right_rows, right_acc = move_rows((right_table, right_state), forward)
    left_full, right_full = (
        lax.all_gather(left_table, "dom", axis=0, tiled=True),
        lax.all_gather(right_rows, "dom", axis=0, tiled=True),
    )
    part_rows = left_full.shape[0]
    width = left_full.shape[1]
    rel_count = relations.shape[0]
    span_count = negatives.shape[0]
    span_len = sources.shape[0] // span_count
    neg_count = negatives.shape[1]
    src_blocks = sources.reshape(span_count, span_len)
    dst_blocks = targets.reshape(span_count, span_len)
    rel_blocks = relation_ids.reshape(span_count, span_len)

    def step(carry, items):
        left_sum, right_sum, rel_sum = carry
        src_rows, dst_rows, rel_rows, neg_rows = items
        left_vec = jnp.take(left_full, src_rows, axis=0)
        right_vec = jnp.take(right_full, dst_rows, axis=0)
        negative = jnp.take(right_full, neg_rows, axis=0)
        operator = jnp.take(relations, rel_rows, axis=0)
        query = left_vec * operator
        positive = jnp.sum(query * right_vec, axis=-1)
        scores = jnp.dot(query, negative.T, precision=high)
        weights = jax.nn.sigmoid(scores - positive[:, None] + margin_gap) / neg_count
        total = jnp.sum(weights, axis=-1)
        grad_query = jnp.dot(weights, negative, precision=high) - total[:, None] * right_vec
        grad_neg = jnp.dot(weights.T, query, precision=high)
        grad_right = -total[:, None] * query
        left_sum = left_sum.at[src_rows].add(grad_query * operator)
        right_sum = right_sum.at[dst_rows].add(grad_right)
        right_sum = right_sum.at[neg_rows].add(grad_neg)
        rel_sum = rel_sum.at[rel_rows].add(grad_query * left_vec)
        return ((left_sum, right_sum, rel_sum), 0)

    start_sums = (
        jnp.zeros((part_rows, width), jnp.float32),
        jnp.zeros((part_rows, width), jnp.float32),
        jnp.zeros((rel_count, width), jnp.float32),
    )
    sums, unused = lax.scan(step, start_sums, (src_blocks, dst_blocks, rel_blocks, negatives))
    left_grad, right_grad, rel_grad = sums
    left_share, right_share = (
        lax.psum_scatter(left_grad, "dom", scatter_dimension=0, tiled=True),
        lax.psum_scatter(right_grad, "dom", scatter_dimension=0, tiled=True),
    )
    new_left, new_left_acc = adagrad(left_table, left_state, left_share)
    new_right_rows, new_right_rows_acc = adagrad(right_rows, right_acc, right_share)
    backward = jnp.mod(-rotation[0], trainers)
    new_right, new_right_acc = move_rows((new_right_rows, new_right_rows_acc), backward)
    rel_total = lax.psum(rel_grad, ("bucket", "dom"))
    new_rel, new_rel_acc = adagrad(relations, relation_state, rel_total)
    return (new_left, new_right, new_left_acc, new_right_acc, new_rel, new_rel_acc)


def solution(mesh):
    return jax.shard_map(
        body,
        mesh=mesh,
        in_specs=(
            P(("bucket", "dom"), None),
            P(("bucket", "dom"), None),
            P(("bucket", "dom")),
            P(("bucket", "dom")),
            P(("bucket", "dom")),
            P(("bucket", "dom")),
            P(("bucket", "dom")),
            P(("bucket", "dom"), None),
            P(),
            P(),
            P(),
        ),
        out_specs=(
            P(("bucket", "dom"), None),
            P(("bucket", "dom"), None),
            P(("bucket", "dom")),
            P(("bucket", "dom")),
            P(),
            P(),
        ),
        check_vma=False,
    )
```

profile of v0, /device:TPU:25, one launch (start us, length us, event | category | flops | bytes accessed | tf_op | source)
XLA Modules:
  0.0 2407.0 jit_solution(12558103134904732058)
XLA Ops:
  8.6 15.2 collective-permute-done
  25.3 24.4 %collective-permute-done.1 = f32[2048,128]{1,0:T(8,128)S(1)} collective-permute-done((f32[2048,128]{1,0:T(8,128)S(1)}, f32[2048,128]{1,0:T(8,128)S(1)}, u32[]{:S(2)}, u32[]{:S(2)}) %collective-permute-start.1) | collective-permute-done | bytes 1048608 | tf_op jit(solution)/shard_map/ppermute | solution.py:12
  49.9 25.7 %collective-permute-done.2 = f32[2048,128]{1,0:T(8,128)S(1)} collective-permute-done((f32[2048,128]{1,0:T(8,128)S(1)}, f32[2048,128]{1,0:T(8,128)S(1)}, u32[]{:S(2)}, u32[]{:S(2)}) %collective-permute-start.2) | collective-permute-done | bytes 1048608 | tf_op jit(solution)/shard_map/ppermute | solution.py:12
  80.8 21.3 collective-permute-done.3
  104.0 23.8 collective-permute-done.4
  129.1 49.3 %all-gather.5.cloned.1.call-done = f32[8192,128]{1,0:T(8,128)} async-done(((f32[2048,128]{1,0:T(8,128)}), f32[8192,128]{1,0:T(8,128)}) %all-gather.5.cloned.1.call-update) | async-done | bytes 4194320 | tf_op jit(solution)/shard_map/all_gather | solution.py:51
  185.2 1910.3 %while.14 = (s32[]{:T(128)}, f32[8192,128]{1,0:T(8,128)}, f32[8192,128]{1,0:T(8,128)}, f32[8192,128]{1,0:T(8,128)}, s32[32,512]{1,0:T(8,128)S(1)}, /*index=5*/f3...) while((s32[]{:T(128)}, f32[8192,128]{1,0:T(8,128)}, ...), condition=%wide.region_7.9_spmd, body=%wide.region_0.8_spmd.sunk | while | flops 2421127680 | bytes 28166792 | solution.py:89
  217.4 10.0 scatter_fusion
  277.1 10.0 scatter_fusion
  396.5 10.0 scatter_fusion
  515.9 10.0 scatter_fusion
  575.6 10.0 scatter_fusion
  635.3 10.0 scatter_fusion
  754.7 10.0 scatter_fusion
  814.4 10.0 scatter_fusion
  874.1 10.0 scatter_fusion
  933.8 10.0 scatter_fusion
  993.5 10.0 scatter_fusion
  1053.2 10.0 scatter_fusion
  1112.9 10.0 scatter_fusion
  1172.6 10.0 scatter_fusion
  1292.0 10.0 scatter_fusion
  1351.7 10.0 scatter_fusion
  1411.4 10.0 scatter_fusion
  1530.8 10.0 scatter_fusion
  1590.4 10.0 scatter_fusion
  2119.8 23.0 reduce-scatter.5.cloned.1.call-done
  2146.7 17.1 collective-permute-done.10
  2164.0 28.6 %collective-permute-done.11 = f32[2048,128]{1,0:T(8,128)S(1)} collective-permute-done((f32[2048,128]{1,0:T(8,128)S(1)}, f32[2048,128]{1,0:T(8,128)S(1)}, u32[]{:S(2)}, u32[]{:S(2)}) %collective-permute-start.11) | collective-permute-done | bytes 1048608 | tf_op jit(solution)/shard_map/ppermute | solution.py:12
  2192.8 127.9 %all-reduce.2.cloned.1.call-done = f32[8192,128]{1,0:T(8,128)} async-done(((f32[8192,128]{1,0:T(8,128)}), f32[8192,128]{1,0:T(8,128)}) %all-reduce.2.cloned.1.call-update) | async-done | bytes 4194320 | tf_op jit(solution)/shard_map/psum | solution.py:99
  2336.7 32.0 %reduce-scatter.3.cloned.1.call-done = f32[2048,128]{1,0:T(8,128)} async-done(((f32[8192,128]{1,0:T(8,128)}), f32[2048,128]{1,0:T(8,128)}) %reduce-scatter.3.cloned.1.call-update) | async-done | bytes 1048592 | tf_op jit(solution)/shard_map/reduce_scatter | solution.py:92
  2378.2 20.6 collective-permute-done.19
  (942 shorter events, 1789.3 us)
Async XLA Ops:
  7.2 121.9 %all-gather.3.cloned.1.call-start = ((), (), s32[]{:S(2)}) async-start(), calls=%async_computation.2 | async-start | bytes 5242880 | tf_op jit(solution)/shard_map/all_gather | solution.py:50
  7.2 16.6 collective-permute-start
  25.2 24.5 %collective-permute-start.1 = (f32[2048,128]{1,0:T(8,128)S(1)}, f32[2048,128]{1,0:T(8,128)S(1)}, u32[]{:S(2)}, u32[]{:S(2)}) collective-permute-start(f32[2048,128]{1,0:T(8,128)S(1)} %broadcast_select_fusion.5), channel_id=1, source_target_pairs={{0,120},{4,124},{8,0},{12,4},{16,8},{20,12},{24,16},{28,20},{32,24... | collective-permute-start | bytes 3145736 | tf_op jit(solution)/shard_map/ppermute | solution.py:12
  25.3 153.2 %all-gather.5.cloned.1.call-start = ((), (), s32[]{:S(2)}) async-start(), calls=%async_computation.3 | async-start | bytes 5242880 | tf_op jit(solution)/shard_map/all_gather | solution.py:51
  49.8 25.8 %collective-permute-start.2 = (f32[2048,128]{1,0:T(8,128)S(1)}, f32[2048,128]{1,0:T(8,128)S(1)}, u32[]{:S(2)}, u32[]{:S(2)}) collective-permute-start(f32[2048,128]{1,0:T(8,128)S(1)} %broadcast_select_fusion.6), channel_id=1, source_target_pairs={{0,112},{4,116},{8,120},{12,124},{16,0},{20,4},{24,8},{28,12},{32,... | collective-permute-start | bytes 3145736 | tf_op jit(solution)/shard_map/ppermute | solution.py:12
  75.7 53.3 %copy-start.4 = (s32[16384]{0:T(1024)S(1)}, s32[16384]{0:T(1024)}, u32[]{:S(2)}) copy-start(s32[16384]{0:T(1024)} %param.19) | copy-start | bytes 196612
  75.7 53.3 %copy-start.5 = (s32[16384]{0:T(1024)S(1)}, s32[16384]{0:T(1024)}, u32[]{:S(2)}) copy-start(s32[16384]{0:T(1024)} %param.21) | copy-start | bytes 196612
  75.7 53.3 %copy-start.6 = (s32[16384]{0:T(1024)S(1)}, s32[16384]{0:T(1024)}, u32[]{:S(2)}) copy-start(s32[16384]{0:T(1024)} %param.20) | copy-start | bytes 196612
  75.7 26.4 %collective-permute-start.3 = (f32[2048,128]{1,0:T(8,128)S(1)}, f32[2048,128]{1,0:T(8,128)S(1)}, u32[]{:S(2)}, u32[]{:S(2)}) collective-permute-start(f32[2048,128]{1,0:T(8,128)S(1)} %broadcast_select_fusion.7), channel_id=1, source_target_pairs={{0,96},{4,100},{8,104},{12,108},{16,112},{20,116},{24,120},{28,124... | collective-permute-start | bytes 3145736 | tf_op jit(solution)/shard_map/ppermute | solution.py:12
  102.2 25.6 %collective-permute-start.4 = (f32[2048,128]{1,0:T(8,128)S(1)}, f32[2048,128]{1,0:T(8,128)S(1)}, u32[]{:S(2)}, u32[]{:S(2)}) collective-permute-start(f32[2048,128]{1,0:T(8,128)S(1)} %broadcast_select_fusion.8), channel_id=1, source_target_pairs={{0,64},{4,68},{8,72},{12,76},{16,80},{20,84},{24,88},{28,92},{32,9... | collective-permute-start | bytes 3145736 | tf_op jit(solution)/shard_map/ppermute | solution.py:12
  128.9 2013.9 %reduce-scatter.5.cloned.1.call-start = ((), (), s32[]{:S(2)}) async-start(), calls=%async_computation.5 | async-start | bytes 5242880 | tf_op jit(solution)/shard_map/reduce_scatter | solution.py:93
  2095.5 225.2 %all-reduce.2.cloned.1.call-start = ((), (), s32[]{:S(2)}) async-start(), calls=%async_computation.6 | async-start | bytes 8388608 | tf_op jit(solution)/shard_map/psum | solution.py:99
  2095.5 48.9 %copy-start.1 = (f32[2048,128]{1,0:T(8,128)S(1)}, f32[2048,128]{1,0:T(8,128)}, u32[]{:S(2)}) copy-start(f32[2048,128]{1,0:T(8,128)} %broadcast_select_fusion.9) | copy-start | bytes 3145732
  2096.0 272.6 %reduce-scatter.3.cloned.1.call-start = ((), (), s32[]{:S(2)}) async-start(), calls=%async_computation.4 | async-start | bytes 5242880 | tf_op jit(solution)/shard_map/reduce_scatter | solution.py:92
  2096.1 5.2 collective-permute-start.5
  2101.4 4.6 collective-permute-start.6
  2106.0 4.9 collective-permute-start.7
  2110.9 7.1 collective-permute-start.8
  2118.0 26.4 %collective-permute-start.9 = (f32[2048]{0:T(1024)S(1)}, f32[2048]{0:T(1024)S(1)}, u32[]{:S(2)}, u32[]{:S(2)}) collective-permute-start(f32[2048]{0:T(1024)S(1)} %broadcast_select_fusion.18), channel_id=1, source_target_pairs={{0,64},{4,68},{8,72},{12,76},{16,80},{20,84},{24,88},{28,92},{32,9... | collective-permute-start | bytes 24584 | tf_op jit(solution)/shard_map/ppermute | solution.py:12
  2146.0 17.8 collective-permute-start.10
  2163.9 160.6 %copy-start.7 = (f32[8192]{0:T(1024)S(1)}, f32[8192]{0:T(1024)}, u32[]{:S(2)}) copy-start(f32[8192]{0:T(1024)} %param.25) | copy-start | bytes 98308
  2163.9 28.7 %collective-permute-start.11 = (f32[2048,128]{1,0:T(8,128)S(1)}, f32[2048,128]{1,0:T(8,128)S(1)}, u32[]{:S(2)}, u32[]{:S(2)}) collective-permute-start(f32[2048,128]{1,0:T(8,128)S(1)} %broadcast_select_fusion), channel_id=1, source_target_pairs={{0,120},{4,124},{8,0},{12,4},{16,8},{20,12},{24,16},{28,20},{32,24... | collective-permute-start | bytes 3145736 | tf_op jit(solution)/shard_map/ppermute | solution.py:12
  2192.7 136.7 %collective-permute-start.12 = (f32[2048,128]{1,0:T(8,128)S(1)}, f32[2048,128]{1,0:T(8,128)S(1)}, u32[]{:S(2)}, u32[]{:S(2)}) collective-permute-start(f32[2048,128]{1,0:T(8,128)S(1)} %broadcast_select_fusion.1), channel_id=1, source_target_pairs={{0,112},{4,116},{8,120},{12,124},{16,0},{20,4},{24,8},{28,12},{32,... | collective-permute-start | bytes 3145736 | tf_op jit(solution)/shard_map/ppermute | solution.py:12
  2324.1 5.3 collective-permute-start.15
  2329.4 7.2 collective-permute-start.16
  2329.5 43.6 %collective-permute-start.13 = (f32[2048,128]{1,0:T(8,128)S(1)}, f32[2048,128]{1,0:T(8,128)S(1)}, u32[]{:S(2)}, u32[]{:S(2)}) collective-permute-start(f32[2048,128]{1,0:T(8,128)S(1)} %broadcast_select_fusion.2), channel_id=1, source_target_pairs={{0,96},{4,100},{8,104},{12,108},{16,112},{20,116},{24,120},{28,124... | collective-permute-start | bytes 3145736 | tf_op jit(solution)/shard_map/ppermute | solution.py:12
  2336.6 37.1 %copy-start.9 = (f32[2048]{0:T(1024)S(1)}, f32[2048]{0:T(1024)}, u32[]{:S(2)}) copy-start(f32[2048]{0:T(1024)} %param.17) | copy-start | bytes 24580
  2336.6 40.3 %copy-start.2 = (f32[2048,128]{1,0:T(8,128)S(1)}, f32[2048,128]{1,0:T(8,128)}, u32[]{:S(2)}) copy-start(f32[2048,128]{1,0:T(8,128)} %param.15) | copy-start | bytes 3145732
  2336.6 33.7 %collective-permute-start.17 = (f32[2048]{0:T(1024)S(1)}, f32[2048]{0:T(1024)S(1)}, u32[]{:S(2)}, u32[]{:S(2)}) collective-permute-start(f32[2048]{0:T(1024)S(1)} %broadcast_select_fusion.11), channel_id=1, source_target_pairs={{0,112},{4,116},{8,120},{12,124},{16,0},{20,4},{24,8},{28,12},{32,... | collective-permute-start | bytes 24584 | tf_op jit(solution)/shard_map/ppermute | solution.py:12
  2370.4 3.9 collective-permute-start.18
  2373.2 26.2 %collective-permute-start.14 = (f32[2048,128]{1,0:T(8,128)S(1)}, f32[2048,128]{1,0:T(8,128)S(1)}, u32[]{:S(2)}, u32[]{:S(2)}) collective-permute-start(f32[2048,128]{1,0:T(8,128)S(1)} %broadcast_select_fusion.3), channel_id=1, source_target_pairs={{0,64},{4,68},{8,72},{12,76},{16,80},{20,84},{24,88},{28,92},{32,9... | collective-permute-start | bytes 3145736 | tf_op jit(solution)/shard_map/ppermute | solution.py:12
  2374.3 24.5 %collective-permute-start.19 = (f32[2048]{0:T(1024)S(1)}, f32[2048]{0:T(1024)S(1)}, u32[]{:S(2)}, u32[]{:S(2)}) collective-permute-start(f32[2048]{0:T(1024)S(1)} %broadcast_select_fusion.13), channel_id=1, source_target_pairs={{0,64},{4,68},{8,72},{12,76},{16,80},{20,84},{24,88},{28,92},{32,9... | collective-permute-start | bytes 24584 | tf_op jit(solution)/shard_map/ppermute | solution.py:12
  (3 other events, 20.6 us)
Sparse Core Ops, SparseCore 0:
  25.4 51.1 all-gather.2
  129.1 49.3 all-gather.4
  2095.6 47.1 reduce-scatter.4
  2148.4 172.2 all-reduce.1
  2323.0 45.6 reduce-scatter.2
where the time goes:
time: 2420 us; the launch traced here: 2410 us
  other arithmetic  1080 us (45%)
  local copies, waits for them, and re-layouts  515 us (21%)
  waiting for transfers between devices  429 us (18%)
  matrix products  340 us (14%)
  starting transfers between devices  26.6 us (1%)
    scatter-add x32, other arithmetic, step(): right_sum = right_sum.at[neg_rows].add(grad_neg)  320 us
    scatter-add x32, other arithmetic, step(): right_sum = right_sum.at[dst_rows].add(grad_right)  234 us
    scatter-add x32, other arithmetic, step(): left_sum = left_sum.at[src_rows].add(grad_query * operator)  233 us
    scatter-add x32, other arithmetic, step(): rel_sum = rel_sum.at[rel_rows].add(grad_query * left_vec)  231 us
    gather x32, local copies, waits for them, and re-layouts, step(): negative = jnp.take(right_full, neg_rows, axis=0)  199 us
    ppermute x20, waiting for transfers between devices, shifted(): lax.ppermute(array, axis, [(i, (i + by) % size) for i in range(size)])  196 us
    dot_general x32, matrix products, step(): grad_neg = jnp.dot(weights.T, query, precision=high)  136 us
    psum x1, waiting for transfers between devices, body(): rel_total = lax.psum(rel_grad, ('bucket', 'dom'))  128 us
  transfers between devices with their start and end apart: 25, of which 17 were waited for; matrix products, arithmetic and copies ran while one was open for 1% of the time, Pallas kernels for 0%

commit v1 on v0

v1 whole, which is shorter than its diff:
```python
import jax
import jax.numpy as jnp
from jax import lax
from jax.experimental import pallas as pl
from jax.experimental.pallas import tpu as pltpu
from jax.sharding import PartitionSpec as P

learn_rate = 0.2
margin_gap = 1.0
TILE = 256
NT = (((1,), (1,)), ((), ()))
NN = (((1,), (0,)), ((), ()))


def adagrad(param, state, grad):
    new_state = state + jnp.mean(grad * grad, axis=-1)
    return (param - learn_rate * grad / jnp.sqrt(new_state)[:, None], new_state)


def rotate(array, amount):
    size = lax.axis_size("bucket")

    def move(by):
        if by == 0:
            return lambda a: a
        return lambda a: lax.ppermute(a, "bucket", [(i, (i - by) % size) for i in range(size)])

    return lax.switch(amount, [move(by) for by in range(size)], array)


def split(a):
    hi = a.astype(jnp.bfloat16)
    return hi, (a - hi.astype(jnp.float32)).astype(jnp.bfloat16)


def dot(a, b, dims=NN):
    return lax.dot_general(a, b, dims, preferred_element_type=jnp.float32)


def local_grads(src, dst, rid, neg, left, right, rel, span_len):
    span_count, neg_count = neg.shape
    neg = neg.reshape(-1)
    width = left.shape[1]
    tile = min(TILE, span_len)
    per = neg_count // span_len

    def kernel(src, dst, rid, neg, left, right, rel, gl, gr, grel, x, r, y, n, gx, gy, gg, gn):
        gl[...] = jnp.zeros_like(gl)
        gr[...] = jnp.zeros_like(gr)
        grel[...] = jnp.zeros_like(grel)

        @pl.loop(0, span_count)
        def _(b):
            @pl.loop(0, span_len // 8)
            def _(i):
                e0 = pl.multiple_of(i * 8, 8)
                n0 = pl.multiple_of(i * 8 * per, 8 * per)
                for s in range(8):
                    e = b * span_len + e0 + s
                    x[pl.ds(e0 + s, 1), :] = left[pl.ds(src[e], 1), :]
                    r[pl.ds(e0 + s, 1), :] = rel[pl.ds(rid[e], 1), :]
                    y[pl.ds(e0 + s, 1), :] = right[pl.ds(dst[e], 1), :]
                    for k in range(per):
                        m = n0 + per * s + k
                        n[pl.ds(m, 1), :] = right[pl.ds(neg[b * neg_count + m], 1), :]

            nh, nl = split(n[...])
            ncat = jnp.concatenate([nh, nl], axis=1)
            acc = jnp.zeros((2 * width, neg_count), jnp.float32)
            acc2 = jnp.zeros((width, neg_count), jnp.float32)
            for t in range(span_len // tile):
                rows = pl.ds(t * tile, tile)
                xv, rv, yv = x[rows, :], r[rows, :], y[rows, :]
                q = xv * rv
                pos = jnp.sum(q * yv, axis=1, keepdims=True)
                qh, ql = split(q)
                score = dot(jnp.concatenate([qh, ql], axis=1), jnp.concatenate([nh, nh], axis=1), NT) + dot(qh, nl, NT)
                w = jax.nn.sigmoid(score + (margin_gap - pos))
                total = jnp.sum(w, axis=1, keepdims=True) * (1.0 / neg_count)
                wh, wl = split(w)
                a = dot(wh, ncat)
                gq = (a[:, :width] + a[:, width:] + dot(wl, nh)) * (1.0 / neg_count) - total * yv
                gx[rows, :] = gq * rv
                gg[rows, :] = gq * xv
                gy[rows, :] = -total * q
                qth, qtl = split(q.T)
                acc += dot(jnp.concatenate([qth, qtl], axis=0), wh)
                acc2 += dot(qth, wl)
            gn[...] = ((acc[:width] + acc[width:] + acc2) * (1.0 / neg_count)).T

            @pl.loop(0, span_len // 8)
            def _(i):
                e0 = pl.multiple_of(i * 8, 8)
                n0 = pl.multiple_of(i * 8 * per, 8 * per)
                for s in range(8):
                    e = b * span_len + e0 + s
                    gl[pl.ds(src[e], 1), :] += gx[pl.ds(e0 + s, 1), :]
                    grel[pl.ds(rid[e], 1), :] += gg[pl.ds(e0 + s, 1), :]
                    gr[pl.ds(dst[e], 1), :] += gy[pl.ds(e0 + s, 1), :]
                    for k in range(per):
                        m = n0 + per * s + k
                        gr[pl.ds(neg[b * neg_count + m], 1), :] += gn[pl.ds(m, 1), :]

    scalars = pl.BlockSpec(memory_space=pltpu.SMEM)
    whole = pl.BlockSpec(memory_space=pltpu.VMEM)
    edge = pltpu.VMEM((span_len, width), jnp.float32)
    negs = pltpu.VMEM((neg_count, width), jnp.float32)
    return pl.pallas_call(
        kernel,
        out_shape=[jax.ShapeDtypeStruct(a.shape, jnp.float32) for a in (left, right, rel)],
        in_specs=[scalars] * 4 + [whole] * 3,
        out_specs=[whole] * 3,
        scratch_shapes=[edge, edge, edge, negs, edge, edge, edge, negs],
        compiler_params=pltpu.CompilerParams(vmem_limit_bytes=60 * 1024 * 1024),
        name="local_grads",
    )(src, dst, rid, neg, left, right, rel)


def body(
    left_table,
    right_table,
    left_state,
    right_state,
    sources,
    targets,
    relation_ids,
    negatives,
    rotation,
    relations,
    relation_state,
):
    trainers = lax.axis_size("bucket")
    left_full = lax.all_gather(left_table, "dom", axis=0, tiled=True)
    right_rows = rotate(right_table, jnp.mod(rotation[0], trainers))
    right_full = lax.all_gather(right_rows, "dom", axis=0, tiled=True)
    span_len = sources.shape[0] // negatives.shape[0]
    left_grad, right_grad, rel_grad = local_grads(
        sources, targets, relation_ids, negatives, left_full, right_full, relations, span_len
    )
    everyone = ("bucket", "dom")
    right_share = lax.psum_scatter(right_grad, "dom", scatter_dimension=0, tiled=True)
    left_share = lax.psum_scatter(left_grad, "dom", scatter_dimension=0, tiled=True)
    right_share = rotate(right_share, jnp.mod(-rotation[0], trainers))
    new_left, new_left_acc = adagrad(left_table, left_state, left_share)
    new_right, new_right_acc = adagrad(right_table, right_state, right_share)
    rel_share = lax.psum_scatter(rel_grad, everyone, scatter_dimension=0, tiled=True)
    rel_total = lax.all_gather(rel_share, everyone, axis=0, tiled=True)
    new_rel, new_rel_acc = adagrad(relations, relation_state, rel_total)
    return (new_left, new_right, new_left_acc, new_right_acc, new_rel, new_rel_acc)


def solution(mesh):
    both = ("bucket", "dom")
    return jax.shard_map(
        body,
        mesh=mesh,
        in_specs=(
            P(both, None),
            P(both, None),
            P(both),
            P(both),
            P(both),
            P(both),
            P(both),
            P(both, None),
            P(),
            P(),
            P(),
        ),
        out_specs=(P(both, None), P(both, None), P(both), P(both), P(), P()),
        check_vma=False,
    )
```

time: 2420 us -> 1270 us (0.52)
  other arithmetic: 1080 us -> 16.7 us
  local copies, waits for them, and re-layouts: 515 us -> 1.71 us
  waiting for transfers between devices: 429 us -> 889 us
  matrix products: 340 us -> 0 us
  Pallas kernels: 0 us -> 333 us
    scatter-add x128 -> x0, other arithmetic: 1020 us -> none  [the longest x32 320 us: step(): right_sum = right_sum.at[neg_rows].add(grad_neg)]
    reduce_scatter x0 -> x1, waiting for transfers between devices: none -> 576 us  [body(): lax.psum_scatter(rel_grad, everyone, scatter_dimension=0, tiled=True)]
    gather x128 -> x0, local copies, waits for them, and re-layouts: 508 us -> none  [the longest x32 199 us: step(): negative = jnp.take(right_full, neg_rows, axis=0)]
    dot_general x96 -> x0, matrix products: 340 us -> none  [the longest x32 136 us: step(): grad_neg = jnp.dot(weights.T, query, precision=high)]
    pallas_call x0 -> x1, Pallas kernels: none -> 333 us  [local_grads(): pl.pallas_call(kernel, out_shape=[jax.ShapeDtypeStruct(a.shape, jnp.float...]
    ppermute x20 -> x2, waiting for transfers between devices: 196 us -> 54.5 us  [move(): lax.ppermute(a, 'bucket', [(i, (i - by) % size) for i in range(size)])]
    psum x1 -> x0, waiting for transfers between devices: 128 us -> none  [body(): rel_total = lax.psum(rel_grad, ('bucket', 'dom'))]
    reduce_scatter x1, waiting for transfers between devices: 23 us -> 110 us  [body(): lax.psum_scatter(right_grad, 'dom', scatter_dimension=0, tiled=True)]
  transfers between devices with their start and end apart: 25 -> 8, of which waited for: 17 -> 8; matrix products, arithmetic and copies ran while one was open for 1% -> 1% of each run, Pallas kernels for 0% -> 0%
where the time goes in v1:
time: 1270 us; the launch traced here: 1260 us
  waiting for transfers between devices  889 us (70%)
  Pallas kernels  333 us (26%)
  other arithmetic  16.7 us (1%)
  between operations  14.9 us (1%)
    reduce_scatter x1, waiting for transfers between devices, body(): lax.psum_scatter(rel_grad, everyone, scatter_dimension=0, tiled=True)  576 us
    pallas_call x1, Pallas kernels, local_grads(): pl.pallas_call(kernel, out_shape=[jax.ShapeDtypeStruct(a.shape, jnp.float...  333 us
    reduce_scatter x1, waiting for transfers between devices, body(): lax.psum_scatter(right_grad, 'dom', scatter_dimension=0, tiled=True)  110 us
    all_gather x1, waiting for transfers between devices, body(): rel_total = lax.all_gather(rel_share, everyone, axis=0, tiled=True)  61.9 us
    ppermute x2, waiting for transfers between devices, move(): lax.ppermute(a, 'bucket', [(i, (i - by) % size) for i in range(size)])  54.5 us
    all_gather x1, waiting for transfers between devices, body(): right_full = lax.all_gather(right_rows, 'dom', axis=0, tiled=True)  50.3 us
  transfers between devices with their start and end apart: 8, of which 8 were waited for; matrix products, arithmetic and copies ran while one was open for 1% of the time, Pallas kernels for 0%

profile of v1, /device:TPU:25, one launch (start us, length us, event | category | flops | bytes accessed | tf_op | source)
XLA Modules:
  0.0 1264.1 jit_solution(11418117246258214995)
XLA Ops:
  7.2 0.7 all-gather.4.cloned.1.call-update
  7.9 0.0 all-gather.6.cloned.1.call-start
  8.6 32.1 %conditional.2 = (f32[2048,128]{1,0:T(8,128)}) conditional(s32[]{:T(128)} %clamp.6, f32[2048,128]{1,0:T(8,128)} %param.76, f32[2048,128]{1,0:T(8,128)} %param.76, f32[2048,128]{1,0:T(8,128)} %param.76, f32[2048,128]{1,0:T(8,128)} %param.76, f32[2048,128]{1,0:T(8,128)} %param.76, f32[2048,128]{1,0:T(8,128)} %param.76, ...), branch_computations={%region_0.1_spmd, %region_1.2_spmd, %region_2.3_spmd, %region_3.4_... | conditional | bytes 4194352 | solution.py:28
  8.7 4.6 collective-permute-start.10
  13.2 27.5 %collective-permute-done.10 = f32[2048,128]{1,0:T(8,128)} collective-permute-done((f32[2048,128]{1,0:T(8,128)}, f32[2048,128]{1,0:T(8,128)}, u32[]{:S(2)}, u32[]{:S(2)}) %collective-permute-start.10) | collective-permute-done | bytes 1048608 | tf_op jit(solution)/shard_map/cond/branch_11_fun/ppermute | solution.py:26
  40.8 0.0 reduce-scatter.8.cloned.1.call-start
  40.8 0.7 copy.17
  41.5 18.6 %all-gather.4.cloned.1.call-done.left = f32[8192,128]{1,0:T(8,128)} async-done(((f32[2048,128]{1,0:T(8,128)}), f32[8192,128]{1,0:T(8,128)}) %all-gather.4.cloned.1.call-update) | async-done | bytes 4194320 | tf_op jit(solution)/shard_map/all_gather | solution.py:133
  60.0 50.3 %all-gather.6.cloned.1.call-done.right = f32[8192,128]{1,0:T(8,128)} async-done(((f32[2048,128]{1,0:T(8,128)}), f32[8192,128]{1,0:T(8,128)}) %all-gather.6.cloned.1.call-update) | async-done | bytes 4194320 | tf_op jit(solution)/shard_map/all_gather | solution.py:135
  110.3 333.2 %local_grads.1 = (f32[8192,128]{1,0:T(8,128)}, f32[8192,128]{1,0:T(8,128)}, f32[8192,128]{1,0:T(8,128)}) custom-call(s32[16384]{0:T(1024)} %src.1, s32[16384]{0:T(1024)} %dst.1, s32[16384]{0:T(1024)} %rid.1, s32[32768]{0:T(1024)} %bitcast.7, f32[8192,128]{1,0:T(8,128)} %all-gather.4.cloned.1.call-done.left, f32[8192,128]{1,0:T(8,128)} %all-gather.6.cloned.1.call-done.right, ...), custom_call_target="tpu_custom_call" | custom-call | tf_op jit(solution)/shard_map/local_grads/pallas_call | solution.py:108
  443.5 0.0 reduce-scatter.6.cloned.1.call-start
  443.6 0.5 reduce-scatter.6.cloned.1.call-update
  444.1 0.0 reduce-scatter.4.cloned.1.call-start
  444.2 0.5 reduce-scatter.4.cloned.1.call-update
  444.7 0.0 all-gather.8.cloned.1.call-start
  444.7 576.2 %reduce-scatter.8.cloned.1.call-done = f32[64,128]{1,0:T(8,128)} async-done(((f32[8192,128]{1,0:T(8,128)}), f32[64,128]{1,0:T(8,128)}) %reduce-scatter.8.cloned.1.call-update) | async-done | bytes 32784 | tf_op jit(solution)/shard_map/reduce_scatter | solution.py:146
  1021.0 109.8 %reduce-scatter.6.cloned.1.call-done = f32[2048,128]{1,0:T(8,128)} async-done(((f32[8192,128]{1,0:T(8,128)}), f32[2048,128]{1,0:T(8,128)}) %reduce-scatter.6.cloned.1.call-update) | async-done | bytes 1048592 | tf_op jit(solution)/shard_map/reduce_scatter | solution.py:141
  1130.9 32.2 %conditional.3 = (f32[2048,128]{1,0:T(8,128)}) conditional(s32[]{:T(128)} %clamp.7, f32[2048,128]{1,0:T(8,128)} %reduce-scatter.6.cloned.1.call-done, f32[2048,128]{1,0:T(8,128)} %reduce-scatter.6.cloned.1.call-done, f32[2048,128]{1,0:T(8,128)} %reduce-scatter.6.cloned.1.call-done, ...), branch_computations={%region_35.36_spmd, %region_36.37_spmd, %region_37.38_spmd, %regio... | conditional | bytes 6291504 | solution.py:28
  1130.9 4.2 collective-permute-start.51
  1135.1 27.0 %collective-permute-done.51 = f32[2048,128]{1,0:T(8,128)S(1)} collective-permute-done((f32[2048,128]{1,0:T(8,128)}, f32[2048,128]{1,0:T(8,128)S(1)}, u32[]{:S(2)}, u32[]{:S(2)}) %collective-permute-start.51) | collective-permute-done | bytes 1048608 | tf_op jit(solution)/shard_map/cond/branch_21_fun/ppermute | solution.py:26
  1162.1 1.0 copy.71
  1163.1 1.7 multiply_reduce_fusion.1
  1164.8 15.5 %reduce-scatter.4.cloned.1.call-done = f32[2048,128]{1,0:T(8,128)} async-done(((f32[8192,128]{1,0:T(8,128)}), f32[2048,128]{1,0:T(8,128)}) %reduce-scatter.4.cloned.1.call-update) | async-done | bytes 1048592 | tf_op jit(solution)/shard_map/reduce_scatter | solution.py:142
  1180.2 1.7 multiply_reduce_fusion.2
  1181.9 0.6 fusion.2
  1182.5 0.6 fusion.1
  1183.1 2.5 divide_subtract_fusion.1
  1185.7 1.3 divide_subtract_fusion.2
  1187.0 61.9 %all-gather.8.cloned.1.call-done = f32[8192,128]{1,0:T(8,128)} async-done(((f32[64,128]{1,0:T(8,128)}), f32[8192,128]{1,0:T(8,128)}) %all-gather.8.cloned.1.call-update) | async-done | bytes 4194320 | tf_op jit(solution)/shard_map/all_gather | solution.py:147
  1248.9 3.5 multiply_reduce_fusion
  1252.4 0.6 fusion
  1253.1 4.2 divide_subtract_fusion
  (20 shorter events, 0.1 us)
Async XLA Ops:
  7.2 33.6 %copy-start.4 = (s32[32,1024]{1,0:T(8,128)S(1)}, s32[32,1024]{1,0:T(8,128)}, u32[]{:S(2)}) copy-start(s32[32,1024]{1,0:T(8,128)} %param.82) | copy-start | bytes 393220
  7.2 52.9 %all-gather.4.cloned.1.call-start = ((), (), s32[]{:S(2)}) async-start(), calls=%async_computation.3 | async-start | bytes 5242880 | tf_op jit(solution)/shard_map/all_gather | solution.py:133
  7.9 102.4 %all-gather.6.cloned.1.call-start = ((), (), s32[]{:S(2)}) async-start(), calls=%async_computation.4 | async-start | bytes 5242880 | tf_op jit(solution)/shard_map/all_gather | solution.py:135
  8.7 32.1 %collective-permute-start.10 = (f32[2048,128]{1,0:T(8,128)}, f32[2048,128]{1,0:T(8,128)}, u32[]{:S(2)}, u32[]{:S(2)}) collective-permute-start(f32[2048,128]{1,0:T(8,128)} %param.11), channel_id=1, source_target_pairs={{0,84},{4,88},{8,92},{12,96},{16,100},{20,104},{24,108},{28,112},{... | collective-permute-start | bytes 3145736 | tf_op jit(solution)/shard_map/cond/branch_11_fun/ppermute | solution.py:26
  40.8 980.2 %reduce-scatter.8.cloned.1.call-start = ((), (), s32[]{:S(2)}) async-start(), calls=%async_computation.7 | async-start | bytes 4227072 | tf_op jit(solution)/shard_map/reduce_scatter | solution.py:146
  443.5 687.3 %reduce-scatter.6.cloned.1.call-start = ((), (), s32[]{:S(2)}) async-start(), calls=%async_computation.6 | async-start | bytes 5242880 | tf_op jit(solution)/shard_map/reduce_scatter | solution.py:141
  444.1 736.1 %reduce-scatter.4.cloned.1.call-start = ((), (), s32[]{:S(2)}) async-start(), calls=%async_computation.5 | async-start | bytes 5242880 | tf_op jit(solution)/shard_map/reduce_scatter | solution.py:142
  444.7 804.2 %all-gather.8.cloned.1.call-start = ((), (), s32[]{:S(2)}) async-start(), calls=%async_computation.8 | async-start | bytes 4227072 | tf_op jit(solution)/shard_map/all_gather | solution.py:147
  1021.0 160.9 %copy-start.6 = (f32[2048]{0:T(1024)S(1)}, f32[2048]{0:T(1024)}, u32[]{:S(2)}) copy-start(f32[2048]{0:T(1024)} %param.77) | copy-start | bytes 24580
  1021.0 161.5 %copy-start.7 = (f32[2048]{0:T(1024)S(1)}, f32[2048]{0:T(1024)}, u32[]{:S(2)}) copy-start(f32[2048]{0:T(1024)} %param.78) | copy-start | bytes 24580
  1021.0 162.1 %copy-start.1 = (f32[2048,128]{1,0:T(8,128)S(1)}, f32[2048,128]{1,0:T(8,128)}, u32[]{:S(2)}) copy-start(f32[2048,128]{1,0:T(8,128)} %param.76) | copy-start | bytes 3145732
  1130.9 31.3 %collective-permute-start.51 = (f32[2048,128]{1,0:T(8,128)}, f32[2048,128]{1,0:T(8,128)S(1)}, u32[]{:S(2)}, u32[]{:S(2)}) collective-permute-start(f32[2048,128]{1,0:T(8,128)} %param.53), channel_id=1, source_target_pairs={{0,44},{4,48},{8,52},{12,56},{16,60},{20,64},{24,68},{28,72},{32,7... | collective-permute-start | bytes 3145736 | tf_op jit(solution)/shard_map/cond/branch_21_fun/ppermute | solution.py:26
  1163.1 22.6 %copy-start.2 = (f32[2048,128]{1,0:T(8,128)S(1)}, f32[2048,128]{1,0:T(8,128)}, u32[]{:S(2)}) copy-start(f32[2048,128]{1,0:T(8,128)} %param.75) | copy-start | bytes 3145732
  1180.2 5.4 copy-start.3
  1185.7 66.8 %copy-start.5 = (f32[8192]{0:T(1024)S(1)}, f32[8192]{0:T(1024)}, u32[]{:S(2)}) copy-start(f32[8192]{0:T(1024)} %param.85) | copy-start | bytes 98308
  1248.9 4.1 copy-start
Sparse Core Ops, SparseCore 0:
  9.7 50.3 all-gather.3
  61.7 48.5 all-gather.5
  443.7 577.2 reduce-scatter.7
  1023.3 107.4 reduce-scatter.5
  1133.7 46.5 reduce-scatter.3
  1183.7 65.1 all-gather.7

commit v2 on v1

--- a/solution.py
+++ b/solution.py
@@ -1,3 +1,5 @@
+import math
+
 import jax
 import jax.numpy as jnp
 from jax import lax
@@ -8,6 +10,10 @@
 learn_rate = 0.2
 margin_gap = 1.0
 TILE = 256
+MESH = pl.DeviceIdType.MESH
+CORES, SIDE = 2, 4
+SIZES = {"core": CORES, "y": SIDE, "z": SIDE, "x": SIDE}
+ORDERS = (("core", "y", "z", "x"), ("core", "z", "y", "x"))
 NT = (((1,), (1,)), ((), ()))
 NN = (((1,), (0,)), ((), ()))
 
@@ -116,6 +122,119 @@
     )(src, dst, rid, neg, left, right, rel)
 
 
+def split_place(bucket):
+    core = lax.rem(bucket, CORES)
+    chip = lax.div(bucket, CORES)
+    return {"core": core, "y": lax.rem(chip, SIDE), "z": lax.div(chip, SIDE), "x": lax.axis_index("dom")}
+
+
+def peer_of(place, axis, by):
+    size = SIZES[axis]
+    spot = dict(place)
+    spot[axis] = lax.rem(place[axis] + by, size)
+    return {"bucket": (spot["z"] * SIDE + spot["y"]) * CORES + spot["core"], "dom": spot["x"]}
+
+
+def sum_everywhere(grads):
+    rows, width = grads.shape
+    half = rows // len(ORDERS)
+
+    def kernel(grad, out, *scratch):
+        levels = len(ORDERS[0])
+        parts = [scratch[k * levels : (k + 1) * levels] for k in range(len(ORDERS))]
+        arrived = [scratch[(len(ORDERS) + k) * levels : (len(ORDERS) + k + 1) * levels] for k in range(len(ORDERS))]
+        send_in, recv_in, send_out, recv_out = scratch[2 * len(ORDERS) * levels :]
+        place = split_place(lax.axis_index("bucket"))
+        barrier = pltpu.get_barrier_semaphore()
+        greeted = 0
+        for axis, size in SIZES.items():
+            for by in range(1, size):
+                pl.semaphore_signal(barrier, inc=1, device_id=peer_of(place, axis, by), device_id_type=MESH)
+                greeted += 1
+        pl.semaphore_wait(barrier, greeted)
+
+        def copy(source, target, sends, recvs, k, level, by, axis):
+            return pltpu.make_async_remote_copy(
+                src_ref=source,
+                dst_ref=target,
+                send_sem=sends.at[k, level, by],
+                recv_sem=recvs.at[k, level, by],
+                device_id=peer_of(place, axis, by),
+                device_id_type=MESH,
+            )
+
+        lows = [k * half for k in range(len(ORDERS))]
+        starts = [[] for _ in ORDERS]
+        for level in range(levels):
+            copies = []
+            for k, order in enumerate(ORDERS):
+                axis = order[level]
+                size = SIZES[axis]
+                block = half // math.prod(SIZES[a] for a in order[: level + 1])
+                source = grad if level == 0 else parts[k][level - 1]
+                base = lows[k] if level == 0 else 0
+                for by in range(1, size):
+                    other = lax.rem(place[axis] + by, size)
+                    c = copy(
+                        source.at[pl.ds(pl.multiple_of(base + other * block, 8), block), :],
+                        arrived[k][level].at[by - 1],
+                        send_in, recv_in, k, level, by, axis,
+                    )
+                    c.start()
+                    copies.append(c)
+            for c in copies:
+                c.wait()
+            for k, order in enumerate(ORDERS):
+                axis = order[level]
+                size = SIZES[axis]
+                block = half // math.prod(SIZES[a] for a in order[: level + 1])
+                source = grad if level == 0 else parts[k][level - 1]
+                base = lows[k] if level == 0 else 0
+                own = source[pl.ds(pl.multiple_of(base + place[axis] * block, 8), block), :]
+                for by in range(1, size):
+                    own = own + arrived[k][level][by - 1]
+                starts[k].append(place[axis] * block)
+                if level < levels - 1:
+                    parts[k][level][...] = own
+                else:
+                    first = lows[k] + sum(starts[k])
+                    out[pl.ds(pl.multiple_of(first, 8), block), :] = own
+        for level in reversed(range(levels)):
+            copies = []
+            for k, order in enumerate(ORDERS):
+                axis = order[level]
+                block = half // math.prod(SIZES[a] for a in order[: level + 1])
+                first = lows[k] + sum(starts[k][: level + 1])
+                where = out.at[pl.ds(pl.multiple_of(first, 8), block), :]
+                for by in range(1, SIZES[axis]):
+                    c = copy(where, where, send_out, recv_out, k, level, by, axis)
+                    c.start()
+                    copies.append(c)
+            for c in copies:
+                c.wait()
+
+    parts, arrived = [], []
+    for order in ORDERS:
+        for level in range(len(order)):
+            block = half // math.prod(SIZES[a] for a in order[: level + 1])
+            parts.append(pltpu.VMEM((block, width), jnp.float32))
+            arrived.append(pltpu.VMEM((SIZES[order[level]] - 1, block, width), jnp.float32))
+    whole = pl.BlockSpec(memory_space=pltpu.VMEM)
+    sems = pltpu.SemaphoreType.DMA((len(ORDERS), len(ORDERS[0]), SIDE))
+    return pl.pallas_call(
+        kernel,
+        out_shape=jax.ShapeDtypeStruct(grads.shape, jnp.float32),
+        in_specs=[whole],
+        out_specs=whole,
+        scratch_shapes=parts + arrived + [sems] * 4,
+        compiler_params=pltpu.CompilerParams(
+            collective_id=0, has_side_effects=True, vmem_limit_bytes=40 * 1024 * 1024
+        ),
+        cost_estimate=pl.CostEstimate(flops=2 * rows * width, bytes_accessed=40 * rows * width, transcendentals=0),
+        name="relation_sums",
+    )(grads)
+
+
 def body(
     left_table,
     right_table,
@@ -137,14 +256,12 @@
     left_grad, right_grad, rel_grad = local_grads(
         sources, targets, relation_ids, negatives, left_full, right_full, relations, span_len
     )
-    everyone = ("bucket", "dom")
     right_share = lax.psum_scatter(right_grad, "dom", scatter_dimension=0, tiled=True)
     left_share = lax.psum_scatter(left_grad, "dom", scatter_dimension=0, tiled=True)
     right_share = rotate(right_share, jnp.mod(-rotation[0], trainers))
     new_left, new_left_acc = adagrad(left_table, left_state, left_share)
     new_right, new_right_acc = adagrad(right_table, right_state, right_share)
-    rel_share = lax.psum_scatter(rel_grad, everyone, scatter_dimension=0, tiled=True)
-    rel_total = lax.all_gather(rel_share, everyone, axis=0, tiled=True)
+    rel_total = sum_everywhere(rel_grad)
     new_rel, new_rel_acc = adagrad(relations, relation_state, rel_total)
     return (new_left, new_right, new_left_acc, new_right_acc, new_rel, new_rel_acc)
 

time: 1270 us -> 561 us (0.44)
  waiting for transfers between devices: 889 us -> 128 us
  Pallas kernels: 333 us -> 393 us
    reduce_scatter x1 -> x0, waiting for transfers between devices: 576 us -> none  [body(): lax.psum_scatter(rel_grad, everyone, scatter_dimension=0, tiled=True)]
    reduce_scatter x1, waiting for transfers between devices: 110 us -> 0.01 us  [body(): lax.psum_scatter(right_grad, 'dom', scatter_dimension=0, tiled=True)]
    all_gather x1 -> x0, waiting for transfers between devices: 61.9 us -> none  [body(): rel_total = lax.all_gather(rel_share, everyone, axis=0, tiled=True)]
    pallas_call x0 -> x1, Pallas kernels: none -> 60.3 us  [sum_everywhere(): pl.pallas_call(kernel, out_shape=jax.ShapeDtypeStruct(grads.shape, jnp.fl...]
    reduce_scatter x1, waiting for transfers between devices: 15.5 us -> 0.01 us  [body(): lax.psum_scatter(left_grad, 'dom', scatter_dimension=0, tiled=True)]
  transfers between devices with their start and end apart: 8 -> 6, of which waited for: 8 -> 4; matrix products, arithmetic and copies ran while one was open for 1% -> 2% of each run, Pallas kernels for 0% -> 11%
where the time goes in v2:
time: 561 us; the launch traced here: 559 us
  Pallas kernels  393 us (70%)
  waiting for transfers between devices  128 us (23%)
  other arithmetic  15.8 us (3%)
  between operations  14.6 us (3%)
    pallas_call x1, Pallas kernels, local_grads(): pl.pallas_call(kernel, out_shape=[jax.ShapeDtypeStruct(a.shape, jnp.float...  333 us
    pallas_call x1, Pallas kernels, sum_everywhere(): pl.pallas_call(kernel, out_shape=jax.ShapeDtypeStruct(grads.shape, jnp.fl...  60.3 us
    ppermute x2, waiting for transfers between devices, move(): lax.ppermute(a, 'bucket', [(i, (i - by) % size) for i in range(size)])  56.1 us
    all_gather x1, waiting for transfers between devices, body(): right_full = lax.all_gather(right_rows, 'dom', axis=0, tiled=True)  50.3 us
    all_gather x1, waiting for transfers between devices, body(): left_full = lax.all_gather(left_table, 'dom', axis=0, tiled=True)  20 us
  transfers between devices with their start and end apart: 6, of which 4 were waited for; matrix products, arithmetic and copies ran while one was open for 2% of the time, Pallas kernels for 11%

profile of v2, /device:TPU:25, one launch (start us, length us, event | category | flops | bytes accessed | tf_op | source)
XLA Modules:
  0.0 559.3 jit_solution(7042822495992202612)
XLA Ops:
  7.2 0.0 all-gather.3.cloned.1.call-start
  7.2 0.7 all-gather.3.cloned.1.call-update
  7.9 0.0 all-gather.5.cloned.1.call-start
  8.6 30.6 %conditional.2 = (f32[2048,128]{1,0:T(8,128)}) conditional(s32[]{:T(128)} %clamp.6, f32[2048,128]{1,0:T(8,128)} %param.76, f32[2048,128]{1,0:T(8,128)} %param.76, f32[2048,128]{1,0:T(8,128)} %param.76, f32[2048,128]{1,0:T(8,128)} %param.76, f32[2048,128]{1,0:T(8,128)} %param.76, f32[2048,128]{1,0:T(8,128)} %param.76, ...), branch_computations={%region_0.1_spmd, %region_1.2_spmd, %region_2.3_spmd, %region_3.4_... | conditional | bytes 4194352 | solution.py:34
  8.7 2.4 collective-permute-start.26
  11.1 28.1 %collective-permute-done.26 = f32[2048,128]{1,0:T(8,128)} collective-permute-done((f32[2048,128]{1,0:T(8,128)}, f32[2048,128]{1,0:T(8,128)}, u32[]{:S(2)}, u32[]{:S(2)}) %collective-permute-start.26) | collective-permute-done | bytes 1048608 | tf_op jit(solution)/shard_map/cond/branch_27_fun/ppermute | solution.py:32
  39.2 0.0 all-gather.5.cloned.1.call-update
  39.3 0.0 reduce-scatter.5.cloned.1.call-start
  39.3 0.7 copy.17
  40.0 20.0 %all-gather.3.cloned.1.call-done.left = f32[8192,128]{1,0:T(8,128)} async-done(((f32[2048,128]{1,0:T(8,128)}), f32[8192,128]{1,0:T(8,128)}) %all-gather.3.cloned.1.call-update) | async-done | bytes 4194320 | tf_op jit(solution)/shard_map/all_gather | solution.py:252
  60.0 50.3 %all-gather.5.cloned.1.call-done.right = f32[8192,128]{1,0:T(8,128)} async-done(((f32[2048,128]{1,0:T(8,128)}), f32[8192,128]{1,0:T(8,128)}) %all-gather.5.cloned.1.call-update) | async-done | bytes 4194320 | tf_op jit(solution)/shard_map/all_gather | solution.py:254
  110.3 333.1 %local_grads.1 = (f32[8192,128]{1,0:T(8,128)}, f32[8192,128]{1,0:T(8,128)}, f32[8192,128]{1,0:T(8,128)}) custom-call(s32[16384]{0:T(1024)} %src.1, s32[16384]{0:T(1024)} %dst.1, s32[16384]{0:T(1024)} %rid.1, s32[32768]{0:T(1024)} %bitcast.7, f32[8192,128]{1,0:T(8,128)} %all-gather.3.cloned.1.call-done.left, f32[8192,128]{1,0:T(8,128)} %all-gather.5.cloned.1.call-done.right, ...), custom_call_target="tpu_custom_call" | custom-call | tf_op jit(solution)/shard_map/local_grads/pallas_call | solution.py:114
  443.4 0.0 reduce-scatter.5.cloned.1.call-update
  443.4 0.0 reduce-scatter.3.cloned.1.call-start
  443.5 0.5 reduce-scatter.3.cloned.1.call-update
  444.1 2.2 copy-done
  446.2 60.3 %relation_sums.1 = f32[8192,128]{1,0:T(8,128)S(1)} custom-call(f32[8192,128]{1,0:T(8,128)S(1)} %copy-done), custom_call_target="tpu_custom_call" | custom-call | flops 2097152 | bytes 41943040 | tf_op jit(solution)/shard_map/relation_sums/pallas_call | solution.py:224
  506.6 0.0 copy-start.5
  506.6 1.2 multiply_reduce_fusion
  507.8 0.6 fusion
  508.4 0.4 copy-done.1
  508.8 4.6 divide_subtract_fusion
  513.4 29.9 %conditional.3 = (f32[2048,128]{1,0:T(8,128)}) conditional(s32[]{:T(128)} %clamp.7, f32[2048,128]{1,0:T(8,128)} %reduce-scatter.5.cloned.1.call-done, f32[2048,128]{1,0:T(8,128)} %reduce-scatter.5.cloned.1.call-done, f32[2048,128]{1,0:T(8,128)} %reduce-scatter.5.cloned.1.call-done, ...), branch_computations={%region_35.36_spmd, %region_36.37_spmd, %region_37.38_spmd, %regio... | conditional | bytes 6291504 | solution.py:34
  513.4 0.9 collective-permute-start.35
  514.3 28.0 %collective-permute-done.35 = f32[2048,128]{1,0:T(8,128)S(1)} collective-permute-done((f32[2048,128]{1,0:T(8,128)}, f32[2048,128]{1,0:T(8,128)S(1)}, u32[]{:S(2)}, u32[]{:S(2)}) %collective-permute-start.35) | collective-permute-done | bytes 1048608 | tf_op jit(solution)/shard_map/cond/branch_5_fun/ppermute | solution.py:32
  542.3 1.0 copy.55
  543.3 1.7 multiply_reduce_fusion.1
  544.9 0.6 fusion.1
  545.5 2.5 divide_subtract_fusion.1
  548.1 1.6 multiply_reduce_fusion.2
  549.7 0.6 fusion.2
  550.3 2.5 divide_subtract_fusion.2
  (15 shorter events, 0.0 us)
Async XLA Ops:
  7.2 32.2 %copy-start.4 = (s32[32,1024]{1,0:T(8,128)S(1)}, s32[32,1024]{1,0:T(8,128)}, u32[]{:S(2)}) copy-start(s32[32,1024]{1,0:T(8,128)} %param.82) | copy-start | bytes 393220
  7.2 52.9 %all-gather.3.cloned.1.call-start = ((), (), s32[]{:S(2)}) async-start(), calls=%async_computation.2 | async-start | bytes 5242880 | tf_op jit(solution)/shard_map/all_gather | solution.py:252
  7.9 102.4 %all-gather.5.cloned.1.call-start = ((), (), s32[]{:S(2)}) async-start(), calls=%async_computation.3 | async-start | bytes 5242880 | tf_op jit(solution)/shard_map/all_gather | solution.py:254
  8.7 30.6 %collective-permute-start.26 = (f32[2048,128]{1,0:T(8,128)}, f32[2048,128]{1,0:T(8,128)}, u32[]{:S(2)}, u32[]{:S(2)}) collective-permute-start(f32[2048,128]{1,0:T(8,128)} %param.27), channel_id=1, source_target_pairs={{0,20},{4,24},{8,28},{12,32},{16,36},{20,40},{24,44},{28,48},{32,5... | collective-permute-start | bytes 3145736 | tf_op jit(solution)/shard_map/cond/branch_27_fun/ppermute | solution.py:32
  39.3 474.1 %reduce-scatter.5.cloned.1.call-start = ((), (), s32[]{:S(2)}) async-start(), calls=%async_computation.5 | async-start | bytes 5242880 | tf_op jit(solution)/shard_map/reduce_scatter | solution.py:259
  443.4 104.6 %reduce-scatter.3.cloned.1.call-start = ((), (), s32[]{:S(2)}) async-start(), calls=%async_computation.4 | async-start | bytes 5242880 | tf_op jit(solution)/shard_map/reduce_scatter | solution.py:260
  444.1 2.2 copy-start
  506.6 1.2 copy-start.5
  506.6 2.2 copy-start.1
  513.4 31.5 %copy-start.6 = (f32[2048]{0:T(1024)S(1)}, f32[2048]{0:T(1024)}, u32[]{:S(2)}) copy-start(f32[2048]{0:T(1024)} %param.78) | copy-start | bytes 24580
  513.4 32.1 %copy-start.2 = (f32[2048,128]{1,0:T(8,128)S(1)}, f32[2048,128]{1,0:T(8,128)}, u32[]{:S(2)}) copy-start(f32[2048,128]{1,0:T(8,128)} %param.76) | copy-start | bytes 3145732
  513.4 28.9 %collective-permute-start.35 = (f32[2048,128]{1,0:T(8,128)}, f32[2048,128]{1,0:T(8,128)S(1)}, u32[]{:S(2)}, u32[]{:S(2)}) collective-permute-start(f32[2048,128]{1,0:T(8,128)} %param.37), channel_id=1, source_target_pairs={{0,108},{4,112},{8,116},{12,120},{16,124},{20,0},{24,4},{28,8},{32... | collective-permute-start | bytes 3145736 | tf_op jit(solution)/shard_map/cond/branch_5_fun/ppermute | solution.py:32
  543.2 6.4 %copy-start.7 = (f32[2048]{0:T(1024)S(1)}, f32[2048]{0:T(1024)}, u32[]{:S(2)}) copy-start(f32[2048]{0:T(1024)} %param.77) | copy-start | bytes 24580
  543.2 7.0 %copy-start.3 = (f32[2048,128]{1,0:T(8,128)S(1)}, f32[2048,128]{1,0:T(8,128)}, u32[]{:S(2)}) copy-start(f32[2048,128]{1,0:T(8,128)} %param.75) | copy-start | bytes 3145732
Sparse Core Ops, SparseCore 0:
  9.7 50.3 all-gather.2
  61.7 48.5 all-gather.4
  443.6 49.9 reduce-scatter.4
  496.0 46.5 reduce-scatter.2

commit v3 on v2

--- a/solution.py
+++ b/solution.py
@@ -10,6 +10,7 @@
 learn_rate = 0.2
 margin_gap = 1.0
 TILE = 256
+VMEM_LIMIT = 60 * 1024 * 1024
 MESH = pl.DeviceIdType.MESH
 CORES, SIDE = 2, 4
 SIZES = {"core": CORES, "y": SIDE, "z": SIDE, "x": SIDE}
@@ -43,33 +44,90 @@
     return lax.dot_general(a, b, dims, preferred_element_type=jnp.float32)
 
 
-def local_grads(src, dst, rid, neg, left, right, rel, span_len):
+def params(**kw):
+    return pltpu.CompilerParams(vmem_limit_bytes=VMEM_LIMIT, **kw)
+
+
+def look_up(src, rid, left, rel, span_len):
+    count = src.shape[0]
+    width = left.shape[1]
+
+    def kernel(src, rid, left, rel, x, r):
+        base = pl.program_id(0) * span_len
+
+        @pl.loop(0, span_len // 16)
+        def _(i):
+            e0 = pl.multiple_of(i * 16, 16)
+            for s in range(16):
+                e = base + e0 + s
+                x[pl.ds(e0 + s, 1), :] = left[pl.ds(src[e], 1), :]
+                r[pl.ds(e0 + s, 1), :] = rel[pl.ds(rid[e], 1), :]
+
+    scalars = pl.BlockSpec(memory_space=pltpu.SMEM)
+    whole = pl.BlockSpec(memory_space=pltpu.VMEM)
+    block = pl.BlockSpec((span_len, width), lambda b: (b, 0))
+    return pl.pallas_call(
+        kernel,
+        grid=(count // span_len,),
+        out_shape=[jax.ShapeDtypeStruct((count, width), jnp.float32)] * 2,
+        in_specs=[scalars] * 2 + [whole] * 2,
+        out_specs=[block] * 2,
+        compiler_params=params(),
+        cost_estimate=pl.CostEstimate(flops=0, bytes_accessed=10 * count * width, transcendentals=0),
+        name="look_up",
+    )(src, rid, left, rel)
+
+
+def score_blocks(src, dst, rid, neg, x, r, right, left_rows, rel_rows, span_len):
     span_count, neg_count = neg.shape
     neg = neg.reshape(-1)
-    width = left.shape[1]
+    count, width = x.shape
     tile = min(TILE, span_len)
     per = neg_count // span_len
 
-    def kernel(src, dst, rid, neg, left, right, rel, gl, gr, grel, x, r, y, n, gx, gy, gg, gn):
-        gl[...] = jnp.zeros_like(gl)
-        gr[...] = jnp.zeros_like(gr)
-        grel[...] = jnp.zeros_like(grel)
-
-        @pl.loop(0, span_count)
-        def _(b):
+    def kernel(src, dst, rid, neg, x, r, right, gl, grel, gy, gn, y, n, gx, gg):
+        b = pl.program_id(0)
+
+        def gather(i):
+            e0 = pl.multiple_of(i * 8, 8)
+            n0 = pl.multiple_of(i * 8 * per, 8 * per)
+            for s in range(8):
+                y[pl.ds(e0 + s, 1), :] = right[pl.ds(dst[b * span_len + e0 + s], 1), :]
+                for k in range(per):
+                    m = n0 + per * s + k
+                    n[pl.ds(m, 1), :] = right[pl.ds(neg[b * neg_count + m], 1), :]
+
+        def scatter(i):
+            e0 = pl.multiple_of(i * 8, 8)
+            for s in range(8):
+                e = (b - 1) * span_len + e0 + s
+                gl[pl.ds(src[e], 1), :] += gx[pl.ds(e0 + s, 1), :]
+                grel[pl.ds(rid[e], 1), :] += gg[pl.ds(e0 + s, 1), :]
+
+        @pl.when(b == 0)
+        def _():
+            gl[...] = jnp.zeros_like(gl)
+            grel[...] = jnp.zeros_like(grel)
+
             @pl.loop(0, span_len // 8)
             def _(i):
-                e0 = pl.multiple_of(i * 8, 8)
-                n0 = pl.multiple_of(i * 8 * per, 8 * per)
-                for s in range(8):
-                    e = b * span_len + e0 + s
-                    x[pl.ds(e0 + s, 1), :] = left[pl.ds(src[e], 1), :]
-                    r[pl.ds(e0 + s, 1), :] = rel[pl.ds(rid[e], 1), :]
-                    y[pl.ds(e0 + s, 1), :] = right[pl.ds(dst[e], 1), :]
-                    for k in range(per):
-                        m = n0 + per * s + k
-                        n[pl.ds(m, 1), :] = right[pl.ds(neg[b * neg_count + m], 1), :]
-
+                gather(i)
+
+        @pl.when((b > 0) & (b < span_count))
+        def _():
+            @pl.loop(0, span_len // 8)
+            def _(i):
+                gather(i)
+                scatter(i)
+
+        @pl.when(b == span_count)
+        def _():
+            @pl.loop(0, span_len // 8)
+            def _(i):
+                scatter(i)
+
+        @pl.when(b < span_count)
+        def _():
             nh, nl = split(n[...])
             ncat = jnp.concatenate([nh, nl], axis=1)
             acc = jnp.zeros((2 * width, neg_count), jnp.float32)
@@ -94,32 +152,79 @@
                 acc2 += dot(qth, wl)
             gn[...] = ((acc[:width] + acc[width:] + acc2) * (1.0 / neg_count)).T
 
-            @pl.loop(0, span_len // 8)
-            def _(i):
-                e0 = pl.multiple_of(i * 8, 8)
-                n0 = pl.multiple_of(i * 8 * per, 8 * per)
-                for s in range(8):
-                    e = b * span_len + e0 + s
-                    gl[pl.ds(src[e], 1), :] += gx[pl.ds(e0 + s, 1), :]
-                    grel[pl.ds(rid[e], 1), :] += gg[pl.ds(e0 + s, 1), :]
-                    gr[pl.ds(dst[e], 1), :] += gy[pl.ds(e0 + s, 1), :]
-                    for k in range(per):
-                        m = n0 + per * s + k
-                        gr[pl.ds(neg[b * neg_count + m], 1), :] += gn[pl.ds(m, 1), :]
-
     scalars = pl.BlockSpec(memory_space=pltpu.SMEM)
     whole = pl.BlockSpec(memory_space=pltpu.VMEM)
-    edge = pltpu.VMEM((span_len, width), jnp.float32)
-    negs = pltpu.VMEM((neg_count, width), jnp.float32)
+    last = span_count - 1
+    edge = pl.BlockSpec((span_len, width), lambda b: (jnp.minimum(b, last), 0))
+    negs = pl.BlockSpec((neg_count, width), lambda b: (jnp.minimum(b, last), 0))
+    edge_rows = pltpu.VMEM((span_len, width), jnp.float32)
+    neg_rows = pltpu.VMEM((neg_count, width), jnp.float32)
     return pl.pallas_call(
         kernel,
-        out_shape=[jax.ShapeDtypeStruct(a.shape, jnp.float32) for a in (left, right, rel)],
-        in_specs=[scalars] * 4 + [whole] * 3,
-        out_specs=[whole] * 3,
-        scratch_shapes=[edge, edge, edge, negs, edge, edge, edge, negs],
-        compiler_params=pltpu.CompilerParams(vmem_limit_bytes=60 * 1024 * 1024),
-        name="local_grads",
-    )(src, dst, rid, neg, left, right, rel)
+        grid=(span_count + 1,),
+        out_shape=[
+            jax.ShapeDtypeStruct(shape, jnp.float32)
+            for shape in ((left_rows, width), (rel_rows, width), (count, width), (neg.shape[0], width))
+        ],
+        in_specs=[scalars] * 4 + [edge] * 2 + [whole],
+        out_specs=[whole] * 2 + [edge, negs],
+        scratch_shapes=[edge_rows, neg_rows, edge_rows, edge_rows],
+        compiler_params=params(),
+        name="score_blocks",
+    )(src, dst, rid, neg, x, r, right)
+
+
+def scatter_right(dst, neg, gy, gn, part_rows, span_len):
+    count, width = gy.shape
+    span_count, neg_count = neg.shape
+    neg = neg.reshape(-1)
+    per = neg_count // span_len
+
+    def kernel(dst, neg, gy, gn, out, odd, neg_even, neg_odd):
+        b = pl.program_id(0)
+        edge_sums, neg_sums = (out, odd), (neg_even, neg_odd)
+
+        @pl.when(b == 0)
+        def _():
+            for a in edge_sums + neg_sums:
+                a[...] = jnp.zeros_like(a)
+
+        @pl.loop(0, span_len // 8)
+        def _(i):
+            e0 = pl.multiple_of(i * 8, 8)
+            n0 = pl.multiple_of(i * 8 * per, 8 * per)
+            for s in range(8):
+                edge_sums[s % 2][pl.ds(dst[b * span_len + e0 + s], 1), :] += gy[pl.ds(e0 + s, 1), :]
+                for k in range(per):
+                    m = n0 + per * s + k
+                    neg_sums[m_parity(s, k, per)][pl.ds(neg[b * neg_count + m], 1), :] += gn[pl.ds(m, 1), :]
+
+        @pl.when(b == span_count - 1)
+        def _():
+            @pl.loop(0, part_rows // 256)
+            def _(i):
+                rows = pl.ds(pl.multiple_of(i * 256, 256), 256)
+                out[rows, :] = (out[rows, :] + odd[rows, :]) + (neg_even[rows, :] + neg_odd[rows, :])
+
+    scalars = pl.BlockSpec(memory_space=pltpu.SMEM)
+    whole = pl.BlockSpec(memory_space=pltpu.VMEM)
+    sums = pltpu.VMEM((part_rows, width), jnp.float32)
+    return pl.pallas_call(
+        kernel,
+        grid=(span_count,),
+        out_shape=jax.ShapeDtypeStruct((part_rows, width), jnp.float32),
+        in_specs=[scalars] * 2
+        + [pl.BlockSpec((span_len, width), lambda b: (b, 0)), pl.BlockSpec((neg_count, width), lambda b: (b, 0))],
+        out_specs=whole,
+        scratch_shapes=[sums] * 3,
+        compiler_params=params(),
+        cost_estimate=pl.CostEstimate(flops=0, bytes_accessed=40 * count * width, transcendentals=0),
+        name="scatter_right",
+    )(dst, neg, gy, gn)
+
+
+def m_parity(s, k, per):
+    return (per * s + k) % 2
 
 
 def split_place(bucket):
@@ -253,11 +358,15 @@
     right_rows = rotate(right_table, jnp.mod(rotation[0], trainers))
     right_full = lax.all_gather(right_rows, "dom", axis=0, tiled=True)
     span_len = sources.shape[0] // negatives.shape[0]
-    left_grad, right_grad, rel_grad = local_grads(
-        sources, targets, relation_ids, negatives, left_full, right_full, relations, span_len
+    part_rows, rel_rows = left_full.shape[0], relations.shape[0]
+    x, r = look_up(sources, relation_ids, left_full, relations, span_len)
+    left_grad, rel_grad, grad_y, grad_n = score_blocks(
+        sources, targets, relation_ids, negatives, x, r, right_full, part_rows, rel_rows, span_len
     )
+    left_share = lax.psum_scatter(left_grad, "dom", scatter_dimension=0, tiled=True)
+    right_grad = scatter_right(targets, negatives, grad_y, grad_n, part_rows, span_len)
+    right_grad, left_share = lax.optimization_barrier((right_grad, left_share))
     right_share = lax.psum_scatter(right_grad, "dom", scatter_dimension=0, tiled=True)
-    left_share = lax.psum_scatter(left_grad, "dom", scatter_dimension=0, tiled=True)
     right_share = rotate(right_share, jnp.mod(-rotation[0], trainers))
     new_left, new_left_acc = adagrad(left_table, left_state, left_share)
     new_right, new_right_acc = adagrad(right_table, right_state, right_share)

time: 561 us -> 510 us (0.909)
  waiting for transfers between devices: 128 us -> 90.2 us
  Pallas kernels: 393 us -> 379 us
    all_gather x1, waiting for transfers between devices: 50.3 us -> 17.9 us  [body(): right_full = lax.all_gather(right_rows, 'dom', axis=0, tiled=True)]
    pallas_call x1 -> x3, Pallas kernels: 333 us -> 319 us  [the longest x1 198 us: score_blocks(): pl.pallas_call(kernel, grid=(span_count + 1,), out_shape=[jax.ShapeDtypeS...]
    ppermute x2, waiting for transfers between devices: 56.1 us -> 48.7 us  [move(): lax.ppermute(a, 'bucket', [(i, (i - by) % size) for i in range(size)])]
  transfers between devices with their start and end apart: 6 -> 6, of which waited for: 4 -> 4; matrix products, arithmetic and copies ran while one was open for 2% -> 2% of each run, Pallas kernels for 11% -> 36%
where the time goes in v3:
time: 510 us; the launch traced here: 508 us
  Pallas kernels  379 us (74%)
  waiting for transfers between devices  90.2 us (18%)
  between operations  14.6 us (3%)
  other arithmetic  13.3 us (3%)
  starting transfers between devices  6.38 us (1%)
    pallas_call x1, Pallas kernels, score_blocks(): pl.pallas_call(kernel, grid=(span_count + 1,), out_shape=[jax.ShapeDtypeS...  198 us
    pallas_call x1, Pallas kernels, scatter_right(): pl.pallas_call(kernel, grid=(span_count,), out_shape=jax.ShapeDtypeStruct...  89.1 us
    pallas_call x1, Pallas kernels, sum_everywhere(): pl.pallas_call(kernel, out_shape=jax.ShapeDtypeStruct(grads.shape, jnp.fl...  60.3 us
    ppermute x2, waiting for transfers between devices, move(): lax.ppermute(a, 'bucket', [(i, (i - by) % size) for i in range(size)])  48.7 us
    pallas_call x1, Pallas kernels, look_up(): pl.pallas_call(kernel, grid=(count // span_len,), out_shape=[jax.ShapeDty...  32.4 us
    all_gather x1, waiting for transfers between devices, body(): left_full = lax.all_gather(left_table, 'dom', axis=0, tiled=True)  22.9 us
    all_gather x1, waiting for transfers between devices, body(): right_full = lax.all_gather(right_rows, 'dom', axis=0, tiled=True)  17.9 us
  transfers between devices with their start and end apart: 6, of which 4 were waited for; matrix products, arithmetic and copies ran while one was open for 2% of the time, Pallas kernels for 36%

profile of v3, /device:TPU:25, one launch (start us, length us, event | category | flops | bytes accessed | tf_op | source)
XLA Modules:
  0.0 508.3 jit_solution(12736613047321051043)
XLA Ops:
  7.2 0.0 all-gather.3.cloned.1.call-start
  7.2 0.7 all-gather.3.cloned.1.call-update
  7.9 0.0 all-gather.5.cloned.1.call-start
  8.6 27.8 %conditional.2 = (f32[2048,128]{1,0:T(8,128)}) conditional(s32[]{:T(128)} %clamp.6, f32[2048,128]{1,0:T(8,128)} %param.76, f32[2048,128]{1,0:T(8,128)} %param.76, f32[2048,128]{1,0:T(8,128)} %param.76, f32[2048,128]{1,0:T(8,128)} %param.76, f32[2048,128]{1,0:T(8,128)} %param.76, f32[2048,128]{1,0:T(8,128)} %param.76, ...), branch_computations={%region_0.1_spmd, %region_1.2_spmd, %region_2.3_spmd, %region_3.4_... | conditional | bytes 4194352 | solution.py:35
  8.7 3.8 collective-permute-start.17
  12.5 23.9 %collective-permute-done.17 = f32[2048,128]{1,0:T(8,128)} collective-permute-done((f32[2048,128]{1,0:T(8,128)}, f32[2048,128]{1,0:T(8,128)}, u32[]{:S(2)}, u32[]{:S(2)}) %collective-permute-start.17) | collective-permute-done | bytes 1048608 | tf_op jit(solution)/shard_map/cond/branch_18_fun/ppermute | solution.py:33
  36.4 0.0 all-gather.5.cloned.1.call-update
  36.4 0.0 reduce-scatter.3.cloned.1.call-start
  36.5 0.7 copy.17
  37.2 22.9 %all-gather.3.cloned.1.call-done.left = f32[8192,128]{1,0:T(8,128)} async-done(((f32[2048,128]{1,0:T(8,128)}), f32[8192,128]{1,0:T(8,128)}) %all-gather.3.cloned.1.call-update) | async-done | bytes 4194320 | tf_op jit(solution)/shard_map/all_gather | solution.py:357
  60.0 32.4 %look_up.1 = (f32[16384,128]{1,0:T(8,128)}, f32[16384,128]{1,0:T(8,128)}) custom-call(s32[16384]{0:T(1024)} %src.3, s32[16384]{0:T(1024)} %rid.3, f32[8192,128]{1,0:T(8,128)} %all-gather.3.cloned.1.call-done.left, f32[8192,128]{1,0:T(8,128)} %rel.1), custom_call_target="tpu_custom_call" | custom-call | bytes 20971520 | tf_op jit(solution)/shard_map/look_up/pallas_call | solution.py:69
  92.5 17.9 %all-gather.5.cloned.1.call-done.right = f32[8192,128]{1,0:T(8,128)} async-done(((f32[2048,128]{1,0:T(8,128)}), f32[8192,128]{1,0:T(8,128)}) %all-gather.5.cloned.1.call-update) | async-done | bytes 4194320 | tf_op jit(solution)/shard_map/all_gather | solution.py:359
  110.3 197.6 %score_blocks.1 = (f32[8192,128]{1,0:T(8,128)}, f32[8192,128]{1,0:T(8,128)}, f32[16384,128]{1,0:T(8,128)}, f32[32768,128]{1,0:T(8,128)}) custom-call(s32[16384]{0:T(1024)} %src.3, s32[16384]{0:T(1024)} %dst.3, s32[16384]{0:T(1024)} %rid.3, s32[32768]{0:T(1024)} %bitcast.7, f32[16384,128]{1,0:T(8,128)} %get-tuple-element.150.x, ...), custom_call_target="tpu_custom_call" | custom-call | tf_op jit(solution)/shard_map/score_blocks/pallas_call | solution.py:162
  307.9 0.0 reduce-scatter.5.cloned.1.call-start
  308.0 89.1 %scatter_right.1 = f32[8192,128]{1,0:T(8,128)} custom-call(s32[16384]{0:T(1024)} %dst.3, s32[32768]{0:T(1024)} %bitcast.8, f32[16384,128]{1,0:T(8,128)} %get-tuple-element.152.gy, f32[32768,128]{1,0:T(8,128)} %get-tuple-element.153.gn), custom_call_target="tpu_custom_call" | custom-call | bytes 83886080 | tf_op jit(solution)/shard_map/scatter_right/pallas_call | solution.py:212
  397.1 0.0 reduce-scatter.5.cloned.1.call-update
  397.1 2.2 copy-done
  399.3 60.3 %relation_sums.1 = f32[8192,128]{1,0:T(8,128)S(1)} custom-call(f32[8192,128]{1,0:T(8,128)S(1)} %copy-done), custom_call_target="tpu_custom_call" | custom-call | flops 2097152 | bytes 41943040 | tf_op jit(solution)/shard_map/relation_sums/pallas_call | solution.py:329
  459.7 1.2 multiply_reduce_fusion
  460.9 0.6 fusion
  461.5 0.4 copy-done.1
  461.9 4.6 divide_subtract_fusion
  466.5 0.3 multiply_reduce_fusion.2
  466.8 0.6 fusion.2
  467.4 1.3 divide_subtract_fusion.2
  468.8 28.2 %conditional.3 = (f32[2048,128]{1,0:T(8,128)}) conditional(s32[]{:T(128)} %clamp.7, f32[2048,128]{1,0:T(8,128)} %reduce-scatter.5.cloned.1.call-done, f32[2048,128]{1,0:T(8,128)} %reduce-scatter.5.cloned.1.call-done, f32[2048,128]{1,0:T(8,128)} %reduce-scatter.5.cloned.1.call-done, ...), branch_computations={%region_35.36_spmd, %region_36.37_spmd, %region_37.38_spmd, %regio... | conditional | bytes 6291504 | solution.py:35
  468.8 2.4 collective-permute-start.44
  471.1 24.9 %collective-permute-done.44 = f32[2048,128]{1,0:T(8,128)S(1)} collective-permute-done((f32[2048,128]{1,0:T(8,128)}, f32[2048,128]{1,0:T(8,128)S(1)}, u32[]{:S(2)}, u32[]{:S(2)}) %collective-permute-start.44) | collective-permute-done | bytes 1048608 | tf_op jit(solution)/shard_map/cond/branch_14_fun/ppermute | solution.py:33
  496.0 1.0 copy.64
  497.0 1.6 multiply_reduce_fusion.1
  498.6 0.6 fusion.1
  499.2 2.5 divide_subtract_fusion.1
  (19 shorter events, 0.1 us)
Async XLA Ops:
  7.2 29.3 %copy-start.5 = (s32[32,1024]{1,0:T(8,128)S(1)}, s32[32,1024]{1,0:T(8,128)}, u32[]{:S(2)}) copy-start(s32[32,1024]{1,0:T(8,128)} %param.82) | copy-start | bytes 393220
  7.2 52.9 %all-gather.3.cloned.1.call-start = ((), (), s32[]{:S(2)}) async-start(), calls=%async_computation.2 | async-start | bytes 5242880 | tf_op jit(solution)/shard_map/all_gather | solution.py:357
  7.9 102.4 %all-gather.5.cloned.1.call-start = ((), (), s32[]{:S(2)}) async-start(), calls=%async_computation.3 | async-start | bytes 5242880 | tf_op jit(solution)/shard_map/all_gather | solution.py:359
  8.7 27.7 %collective-permute-start.17 = (f32[2048,128]{1,0:T(8,128)}, f32[2048,128]{1,0:T(8,128)}, u32[]{:S(2)}, u32[]{:S(2)}) collective-permute-start(f32[2048,128]{1,0:T(8,128)} %param.18), channel_id=1, source_target_pairs={{0,56},{4,60},{8,64},{12,68},{16,72},{20,76},{24,80},{28,84},{32,8... | collective-permute-start | bytes 3145736 | tf_op jit(solution)/shard_map/cond/branch_18_fun/ppermute | solution.py:33
  36.4 360.7 %reduce-scatter.3.cloned.1.call-start = ((), (), s32[]{:S(2)}) async-start(), calls=%async_computation.4 | async-start | bytes 5242880 | tf_op jit(solution)/shard_map/reduce_scatter | solution.py:366
  307.9 160.9 %reduce-scatter.5.cloned.1.call-start = ((), (), s32[]{:S(2)}) async-start(), calls=%async_computation.5 | async-start | bytes 5242880 | tf_op jit(solution)/shard_map/reduce_scatter | solution.py:369
  397.1 2.2 copy-start
  459.7 1.2 copy-start.6
  459.7 2.2 copy-start.1
  461.9 4.6 copy-start.4
  461.9 4.9 copy-start.7
  461.9 5.5 %copy-start.2 = (f32[2048,128]{1,0:T(8,128)S(1)}, f32[2048,128]{1,0:T(8,128)}, u32[]{:S(2)}) copy-start(f32[2048,128]{1,0:T(8,128)} %param.75) | copy-start | bytes 3145732
  468.8 29.8 %copy-start.8 = (f32[2048]{0:T(1024)S(1)}, f32[2048]{0:T(1024)}, u32[]{:S(2)}) copy-start(f32[2048]{0:T(1024)} %param.78) | copy-start | bytes 24580
  468.8 30.4 %copy-start.3 = (f32[2048,128]{1,0:T(8,128)S(1)}, f32[2048,128]{1,0:T(8,128)}, u32[]{:S(2)}) copy-start(f32[2048,128]{1,0:T(8,128)} %param.76) | copy-start | bytes 3145732
  468.8 27.2 %collective-permute-start.44 = (f32[2048,128]{1,0:T(8,128)}, f32[2048,128]{1,0:T(8,128)S(1)}, u32[]{:S(2)}, u32[]{:S(2)}) collective-permute-start(f32[2048,128]{1,0:T(8,128)} %param.46), channel_id=1, source_target_pairs={{0,72},{4,76},{8,80},{12,84},{16,88},{20,92},{24,96},{28,100},{32,... | collective-permute-start | bytes 3145736 | tf_op jit(solution)/shard_map/cond/branch_14_fun/ppermute | solution.py:33
Sparse Core Ops, SparseCore 0:
  9.7 50.3 all-gather.2
  61.7 48.5 all-gather.4
  308.0 47.1 reduce-scatter.2
  397.2 49.9 reduce-scatter.4

commit v4 on v3

--- a/solution.py
+++ b/solution.py
@@ -10,6 +10,9 @@
 learn_rate = 0.2
 margin_gap = 1.0
 TILE = 256
+UNROLL = 32
+SUMS = 2
+NEG_SUMS = 4
 VMEM_LIMIT = 60 * 1024 * 1024
 MESH = pl.DeviceIdType.MESH
 CORES, SIDE = 2, 4
@@ -78,6 +81,16 @@
     )(src, rid, left, rel)
 
 
+def fold(sums):
+    @pl.loop(0, sums[0].shape[0] // 256)
+    def _(i):
+        rows = pl.ds(pl.multiple_of(i * 256, 256), 256)
+        total = sums[0][rows, :]
+        for a in sums[1:]:
+            total = total + a[rows, :]
+        sums[0][rows, :] = total
+
+
 def score_blocks(src, dst, rid, neg, x, r, right, left_rows, rel_rows, span_len):
     span_count, neg_count = neg.shape
     neg = neg.reshape(-1)
@@ -85,46 +98,53 @@
     tile = min(TILE, span_len)
     per = neg_count // span_len
 
-    def kernel(src, dst, rid, neg, x, r, right, gl, grel, gy, gn, y, n, gx, gg):
+    def kernel(src, dst, rid, neg, x, r, right_hbm, gl_hbm, grel_hbm, gy, gn, right, y, n, gx, gg, sems, *sums):
         b = pl.program_id(0)
-
-        def gather(i):
-            e0 = pl.multiple_of(i * 8, 8)
-            n0 = pl.multiple_of(i * 8 * per, 8 * per)
-            for s in range(8):
-                y[pl.ds(e0 + s, 1), :] = right[pl.ds(dst[b * span_len + e0 + s], 1), :]
-                for k in range(per):
-                    m = n0 + per * s + k
-                    n[pl.ds(m, 1), :] = right[pl.ds(neg[b * neg_count + m], 1), :]
-
-        def scatter(i):
-            e0 = pl.multiple_of(i * 8, 8)
-            for s in range(8):
-                e = (b - 1) * span_len + e0 + s
-                gl[pl.ds(src[e], 1), :] += gx[pl.ds(e0 + s, 1), :]
-                grel[pl.ds(rid[e], 1), :] += gg[pl.ds(e0 + s, 1), :]
+        left_sums, rel_sums = sums[:SUMS], sums[SUMS:]
+
+        def move_rows(i, gathers, scatters):
+            e0 = pl.multiple_of(i * UNROLL, UNROLL)
+            n0 = pl.multiple_of(i * UNROLL * per, UNROLL * per)
+            now, before = b * span_len + e0, (b - 1) * span_len + e0
+            for s in range(UNROLL):
+                if scatters:
+                    left_sums[s % SUMS][pl.ds(src[before + s], 1), :] += gx[pl.ds(e0 + s, 1), :]
+                    rel_sums[s % SUMS][pl.ds(rid[before + s], 1), :] += gg[pl.ds(e0 + s, 1), :]
+                if gathers:
+                    y[pl.ds(e0 + s, 1), :] = right[pl.ds(dst[now + s], 1), :]
+                    for m in range(per * s, per * s + per):
+                        n[pl.ds(n0 + m, 1), :] = right[pl.ds(neg[b * neg_count + n0 + m], 1), :]
+
+        def every_row(gathers, scatters):
+            @pl.loop(0, span_len // UNROLL)
+            def _(i):
+                move_rows(i, gathers, scatters)
 
         @pl.when(b == 0)
         def _():
-            gl[...] = jnp.zeros_like(gl)
-            grel[...] = jnp.zeros_like(grel)
-
-            @pl.loop(0, span_len // 8)
-            def _(i):
-                gather(i)
+            copy = pltpu.make_async_copy(right_hbm, right, sems.at[0])
+            copy.start()
+            for a in left_sums + rel_sums:
+                a[...] = jnp.zeros_like(a)
+            copy.wait()
+
+            every_row(True, False)
 
         @pl.when((b > 0) & (b < span_count))
         def _():
-            @pl.loop(0, span_len // 8)
-            def _(i):
-                gather(i)
-                scatter(i)
+            every_row(True, True)
 
         @pl.when(b == span_count)
         def _():
-            @pl.loop(0, span_len // 8)
-            def _(i):
-                scatter(i)
+            every_row(False, True)
+            fold(left_sums)
+            fold(rel_sums)
+            left_copy = pltpu.make_async_copy(left_sums[0], gl_hbm, sems.at[0])
+            rel_copy = pltpu.make_async_copy(rel_sums[0], grel_hbm, sems.at[1])
+            left_copy.start()
+            rel_copy.start()
+            left_copy.wait()
+            rel_copy.wait()
 
         @pl.when(b < span_count)
         def _():
@@ -153,7 +173,7 @@
             gn[...] = ((acc[:width] + acc[width:] + acc2) * (1.0 / neg_count)).T
 
     scalars = pl.BlockSpec(memory_space=pltpu.SMEM)
-    whole = pl.BlockSpec(memory_space=pltpu.VMEM)
+    anywhere = pl.BlockSpec(memory_space=pl.ANY)
     last = span_count - 1
     edge = pl.BlockSpec((span_len, width), lambda b: (jnp.minimum(b, last), 0))
     negs = pl.BlockSpec((neg_count, width), lambda b: (jnp.minimum(b, last), 0))
@@ -166,9 +186,18 @@
             jax.ShapeDtypeStruct(shape, jnp.float32)
             for shape in ((left_rows, width), (rel_rows, width), (count, width), (neg.shape[0], width))
         ],
-        in_specs=[scalars] * 4 + [edge] * 2 + [whole],
-        out_specs=[whole] * 2 + [edge, negs],
-        scratch_shapes=[edge_rows, neg_rows, edge_rows, edge_rows],
+        in_specs=[scalars] * 4 + [edge] * 2 + [anywhere],
+        out_specs=[anywhere] * 2 + [edge, negs],
+        scratch_shapes=[
+            pltpu.VMEM(right.shape, jnp.float32),
+            edge_rows,
+            neg_rows,
+            edge_rows,
+            edge_rows,
+            pltpu.SemaphoreType.DMA((2,)),
+        ]
+        + [pltpu.VMEM((left_rows, width), jnp.float32)] * SUMS
+        + [pltpu.VMEM((rel_rows, width), jnp.float32)] * SUMS,
         compiler_params=params(),
         name="score_blocks",
     )(src, dst, rid, neg, x, r, right)
@@ -180,34 +209,36 @@
     neg = neg.reshape(-1)
     per = neg_count // span_len
 
-    def kernel(dst, neg, gy, gn, out, odd, neg_even, neg_odd):
+    def kernel(dst, neg, gy_block, gn_block, out, gy, gn, *sums_sem):
+        *sums, sem = sums_sem
         b = pl.program_id(0)
-        edge_sums, neg_sums = (out, odd), (neg_even, neg_odd)
+        edge_sums, neg_sums = sums[:2], sums[2:]
+        gy[...] = gy_block[...]
+        gn[...] = gn_block[...]
 
         @pl.when(b == 0)
         def _():
-            for a in edge_sums + neg_sums:
+            for a in sums:
                 a[...] = jnp.zeros_like(a)
 
-        @pl.loop(0, span_len // 8)
+        @pl.loop(0, span_len // UNROLL)
         def _(i):
-            e0 = pl.multiple_of(i * 8, 8)
-            n0 = pl.multiple_of(i * 8 * per, 8 * per)
-            for s in range(8):
+            e0 = pl.multiple_of(i * UNROLL, UNROLL)
+            n0 = pl.multiple_of(i * UNROLL * per, UNROLL * per)
+            for s in range(UNROLL):
                 edge_sums[s % 2][pl.ds(dst[b * span_len + e0 + s], 1), :] += gy[pl.ds(e0 + s, 1), :]
                 for k in range(per):
                     m = n0 + per * s + k
-                    neg_sums[m_parity(s, k, per)][pl.ds(neg[b * neg_count + m], 1), :] += gn[pl.ds(m, 1), :]
+                    neg_sums[(per * s + k) % len(neg_sums)][pl.ds(neg[b * neg_count + m], 1), :] += gn[pl.ds(m, 1), :]
 
         @pl.when(b == span_count - 1)
         def _():
-            @pl.loop(0, part_rows // 256)
-            def _(i):
-                rows = pl.ds(pl.multiple_of(i * 256, 256), 256)
-                out[rows, :] = (out[rows, :] + odd[rows, :]) + (neg_even[rows, :] + neg_odd[rows, :])
+            fold(sums)
+            copy = pltpu.make_async_copy(sums[0], out, sem)
+            copy.start()
+            copy.wait()
 
     scalars = pl.BlockSpec(memory_space=pltpu.SMEM)
-    whole = pl.BlockSpec(memory_space=pltpu.VMEM)
     sums = pltpu.VMEM((part_rows, width), jnp.float32)
     return pl.pallas_call(
         kernel,
@@ -215,16 +246,14 @@
         out_shape=jax.ShapeDtypeStruct((part_rows, width), jnp.float32),
         in_specs=[scalars] * 2
         + [pl.BlockSpec((span_len, width), lambda b: (b, 0)), pl.BlockSpec((neg_count, width), lambda b: (b, 0))],
-        out_specs=whole,
-        scratch_shapes=[sums] * 3,
+        out_specs=pl.BlockSpec(memory_space=pl.ANY),
+        scratch_shapes=[pltpu.VMEM((span_len, width), jnp.float32), pltpu.VMEM((neg_count, width), jnp.float32)]
+        + [sums] * (2 + NEG_SUMS)
+        + [pltpu.SemaphoreType.DMA],
         compiler_params=params(),
         cost_estimate=pl.CostEstimate(flops=0, bytes_accessed=40 * count * width, transcendentals=0),
         name="scatter_right",
     )(dst, neg, gy, gn)
-
-
-def m_parity(s, k, per):
-    return (per * s + k) % 2
 
 
 def split_place(bucket):

time: 510 us -> 435 us (0.85)
  Pallas kernels: 379 us -> 303 us
    pallas_call x1, Pallas kernels: 198 us -> 148 us  [score_blocks(): pl.pallas_call(kernel, grid=(span_count + 1,), out_shape=[jax.ShapeDtypeS...]
    pallas_call x1, Pallas kernels: 89.1 us -> 62.3 us  [scatter_right(): pl.pallas_call(kernel, grid=(span_count,), out_shape=jax.ShapeDtypeStruct...]
where the time goes in v4:
time: 435 us; the launch traced here: 433 us
  Pallas kernels  303 us (70%)
  waiting for transfers between devices  92.7 us (21%)
  between operations  14.6 us (3%)
  other arithmetic  13.3 us (3%)
  starting transfers between devices  4.89 us (1%)
    pallas_call x1, Pallas kernels, score_blocks(): pl.pallas_call(kernel, grid=(span_count + 1,), out_shape=[jax.ShapeDtypeS...  148 us
    pallas_call x1, Pallas kernels, scatter_right(): pl.pallas_call(kernel, grid=(span_count,), out_shape=jax.ShapeDtypeStruct...  62.3 us
    pallas_call x1, Pallas kernels, sum_everywhere(): pl.pallas_call(kernel, out_shape=jax.ShapeDtypeStruct(grads.shape, jnp.fl...  60.3 us
    ppermute x2, waiting for transfers between devices, move(): lax.ppermute(a, 'bucket', [(i, (i - by) % size) for i in range(size)])  50.2 us
    pallas_call x1, Pallas kernels, look_up(): pl.pallas_call(kernel, grid=(count // span_len,), out_shape=[jax.ShapeDty...  32.4 us
    all_gather x1, waiting for transfers between devices, body(): left_full = lax.all_gather(left_table, 'dom', axis=0, tiled=True)  23.8 us
    all_gather x1, waiting for transfers between devices, body(): right_full = lax.all_gather(right_rows, 'dom', axis=0, tiled=True)  17.9 us
  transfers between devices with their start and end apart: 6, of which 4 were waited for; matrix products, arithmetic and copies ran while one was open for 2% of the time, Pallas kernels for 36%

profile of v4, /device:TPU:25, one launch (start us, length us, event | category | flops | bytes accessed | tf_op | source)
XLA Modules:
  0.0 433.1 jit_solution(14337110534981511812)
XLA Ops:
  7.2 0.0 all-gather.3.cloned.1.call-start
  7.2 0.7 all-gather.3.cloned.1.call-update
  7.9 0.0 all-gather.5.cloned.1.call-start
  8.6 26.9 %conditional.2 = (f32[2048,128]{1,0:T(8,128)}) conditional(s32[]{:T(128)} %clamp.6, f32[2048,128]{1,0:T(8,128)} %param.76, f32[2048,128]{1,0:T(8,128)} %param.76, f32[2048,128]{1,0:T(8,128)} %param.76, f32[2048,128]{1,0:T(8,128)} %param.76, f32[2048,128]{1,0:T(8,128)} %param.76, f32[2048,128]{1,0:T(8,128)} %param.76, ...), branch_computations={%region_0.1_spmd, %region_1.2_spmd, %region_2.3_spmd, %region_3.4_... | conditional | bytes 4194352 | solution.py:38
  8.7 3.5 collective-permute-start.13
  12.2 23.3 %collective-permute-done.13 = f32[2048,128]{1,0:T(8,128)} collective-permute-done((f32[2048,128]{1,0:T(8,128)}, f32[2048,128]{1,0:T(8,128)}, u32[]{:S(2)}, u32[]{:S(2)}) %collective-permute-start.13) | collective-permute-done | bytes 1048608 | tf_op jit(solution)/shard_map/cond/branch_14_fun/ppermute | solution.py:36
  35.5 0.0 all-gather.5.cloned.1.call-update
  35.5 0.0 reduce-scatter.3.cloned.1.call-start
  35.6 0.7 copy.17
  36.2 23.8 %all-gather.3.cloned.1.call-done.left = f32[8192,128]{1,0:T(8,128)} async-done(((f32[2048,128]{1,0:T(8,128)}), f32[8192,128]{1,0:T(8,128)}) %all-gather.3.cloned.1.call-update) | async-done | bytes 4194320 | tf_op jit(solution)/shard_map/all_gather | solution.py:386
  60.0 32.4 %look_up.1 = (f32[16384,128]{1,0:T(8,128)}, f32[16384,128]{1,0:T(8,128)}) custom-call(s32[16384]{0:T(1024)} %src.3, s32[16384]{0:T(1024)} %rid.3, f32[8192,128]{1,0:T(8,128)} %all-gather.3.cloned.1.call-done.left, f32[8192,128]{1,0:T(8,128)} %rel.1), custom_call_target="tpu_custom_call" | custom-call | bytes 20971520 | tf_op jit(solution)/shard_map/look_up/pallas_call | solution.py:72
  92.5 17.9 %all-gather.5.cloned.1.call-done.right_hbm = f32[8192,128]{1,0:T(8,128)} async-done(((f32[2048,128]{1,0:T(8,128)}), f32[8192,128]{1,0:T(8,128)}) %all-gather.5.cloned.1.call-update) | async-done | bytes 4194320 | tf_op jit(solution)/shard_map/all_gather | solution.py:388
  110.3 148.2 %score_blocks.1 = (f32[8192,128]{1,0:T(8,128)}, f32[8192,128]{1,0:T(8,128)}, f32[16384,128]{1,0:T(8,128)}, f32[32768,128]{1,0:T(8,128)}) custom-call(s32[16384]{0:T(1024)} %src.3, s32[16384]{0:T(1024)} %dst.3, s32[16384]{0:T(1024)} %rid.3, s32[32768]{0:T(1024)} %bitcast.7, f32[16384,128]{1,0:T(8,128)} %get-tuple-element.150.x, ...), custom_call_target="tpu_custom_call" | custom-call | tf_op jit(solution)/shard_map/score_blocks/pallas_call | solution.py:182
  258.6 0.0 reduce-scatter.5.cloned.1.call-start
  258.7 62.3 %scatter_right.1 = f32[8192,128]{1,0:T(8,128)} custom-call(s32[16384]{0:T(1024)} %dst.3, s32[32768]{0:T(1024)} %bitcast.8, f32[16384,128]{1,0:T(8,128)} %get-tuple-element.152.gy_block, f32[32768,128]{1,0:T(8,128)} %get-tuple-element.153.gn_block), custom_call_target="tpu_custom_call" | custom-call | bytes 83886080 | tf_op jit(solution)/shard_map/scatter_right/pallas_call | solution.py:243
  321.0 0.0 reduce-scatter.3.cloned.1.call-done
  321.1 2.2 copy-done
  323.3 60.3 %relation_sums.1 = f32[8192,128]{1,0:T(8,128)S(1)} custom-call(f32[8192,128]{1,0:T(8,128)S(1)} %copy-done), custom_call_target="tpu_custom_call" | custom-call | flops 2097152 | bytes 41943040 | tf_op jit(solution)/shard_map/relation_sums/pallas_call | solution.py:358
  383.6 1.2 multiply_reduce_fusion
  384.8 0.6 fusion
  385.4 0.4 copy-done.1
  385.8 4.6 %divide_subtract_fusion = f32[8192,128]{1,0:T(8,128)} fusion(f32[8192,128]{1,0:T(8,128)S(1)} %copy-done.1, f32[8192,128]{1,0:T(8,128)S(1)} %relation_sums.1, f32[8192]{0:T(1024)S(1)} %get-tuple-element.158), kind=kLoop, calls=%fused_computation | loop fusion | flops 3145728 | bytes 12615680 | tf_op jit(solution)/shard_map/sub | solution.py:27
  390.4 0.3 multiply_reduce_fusion.2
  390.8 0.6 fusion.2
  391.4 1.3 divide_subtract_fusion.2
  392.7 29.2 %conditional.3 = (f32[2048,128]{1,0:T(8,128)}) conditional(s32[]{:T(128)} %clamp.7, f32[2048,128]{1,0:T(8,128)} %reduce-scatter.5.cloned.1.call-done, f32[2048,128]{1,0:T(8,128)} %reduce-scatter.5.cloned.1.call-done, f32[2048,128]{1,0:T(8,128)} %reduce-scatter.5.cloned.1.call-done, ...), branch_computations={%region_35.36_spmd, %region_36.37_spmd, %region_37.38_spmd, %regio... | conditional | bytes 6291504 | solution.py:38
  392.7 1.2 collective-permute-start.48
  393.9 26.9 %collective-permute-done.48 = f32[2048,128]{1,0:T(8,128)S(1)} collective-permute-done((f32[2048,128]{1,0:T(8,128)}, f32[2048,128]{1,0:T(8,128)S(1)}, u32[]{:S(2)}, u32[]{:S(2)}) %collective-permute-start.48) | collective-permute-done | bytes 1048608 | tf_op jit(solution)/shard_map/cond/branch_18_fun/ppermute | solution.py:36
  420.8 1.0 copy.68
  421.8 1.6 multiply_reduce_fusion.1
  423.4 0.6 fusion.1
  424.0 2.5 divide_subtract_fusion.1
  (19 shorter events, 0.1 us)
Async XLA Ops:
  7.2 28.4 %copy-start.5 = (s32[32,1024]{1,0:T(8,128)S(1)}, s32[32,1024]{1,0:T(8,128)}, u32[]{:S(2)}) copy-start(s32[32,1024]{1,0:T(8,128)} %param.82) | copy-start | bytes 393220
  7.2 52.9 %all-gather.3.cloned.1.call-start = ((), (), s32[]{:S(2)}) async-start(), calls=%async_computation.2 | async-start | bytes 5242880 | tf_op jit(solution)/shard_map/all_gather | solution.py:386
  7.9 102.4 %all-gather.5.cloned.1.call-start = ((), (), s32[]{:S(2)}) async-start(), calls=%async_computation.3 | async-start | bytes 5242880 | tf_op jit(solution)/shard_map/all_gather | solution.py:388
  8.7 26.8 %collective-permute-start.13 = (f32[2048,128]{1,0:T(8,128)}, f32[2048,128]{1,0:T(8,128)}, u32[]{:S(2)}, u32[]{:S(2)}) collective-permute-start(f32[2048,128]{1,0:T(8,128)} %param.14), channel_id=1, source_target_pairs={{0,72},{4,76},{8,80},{12,84},{16,88},{20,92},{24,96},{28,100},{32,... | collective-permute-start | bytes 3145736 | tf_op jit(solution)/shard_map/cond/branch_14_fun/ppermute | solution.py:36
  35.5 285.5 %reduce-scatter.3.cloned.1.call-start = ((), (), s32[]{:S(2)}) async-start(), calls=%async_computation.4 | async-start | bytes 5242880 | tf_op jit(solution)/shard_map/reduce_scatter | solution.py:395
  258.6 134.1 %reduce-scatter.5.cloned.1.call-start = ((), (), s32[]{:S(2)}) async-start(), calls=%async_computation.5 | async-start | bytes 5242880 | tf_op jit(solution)/shard_map/reduce_scatter | solution.py:398
  321.1 2.2 copy-start
  383.6 1.2 copy-start.6
  383.6 2.2 copy-start.1
  385.8 4.6 %copy-start.4 = (f32[2048,128]{1,0:T(8,128)S(1)}, f32[2048,128]{1,0:T(8,128)}, u32[]{:S(2)}) copy-start(f32[2048,128]{1,0:T(8,128)} %reduce-scatter.3.cloned.1.call-done) | copy-start | bytes 3145732
  385.8 4.9 %copy-start.7 = (f32[2048]{0:T(1024)S(1)}, f32[2048]{0:T(1024)}, u32[]{:S(2)}) copy-start(f32[2048]{0:T(1024)} %param.77) | copy-start | bytes 24580
  385.8 5.5 %copy-start.2 = (f32[2048,128]{1,0:T(8,128)S(1)}, f32[2048,128]{1,0:T(8,128)}, u32[]{:S(2)}) copy-start(f32[2048,128]{1,0:T(8,128)} %param.75) | copy-start | bytes 3145732
  392.7 30.7 %copy-start.8 = (f32[2048]{0:T(1024)S(1)}, f32[2048]{0:T(1024)}, u32[]{:S(2)}) copy-start(f32[2048]{0:T(1024)} %param.78) | copy-start | bytes 24580
  392.7 31.3 %copy-start.3 = (f32[2048,128]{1,0:T(8,128)S(1)}, f32[2048,128]{1,0:T(8,128)}, u32[]{:S(2)}) copy-start(f32[2048,128]{1,0:T(8,128)} %param.76) | copy-start | bytes 3145732
  392.7 28.2 %collective-permute-start.48 = (f32[2048,128]{1,0:T(8,128)}, f32[2048,128]{1,0:T(8,128)S(1)}, u32[]{:S(2)}, u32[]{:S(2)}) collective-permute-start(f32[2048,128]{1,0:T(8,128)} %param.50), channel_id=1, source_target_pairs={{0,56},{4,60},{8,64},{12,68},{16,72},{20,76},{24,80},{28,84},{32,8... | collective-permute-start | bytes 3145736 | tf_op jit(solution)/shard_map/cond/branch_18_fun/ppermute | solution.py:36
Sparse Core Ops, SparseCore 0:
  9.7 50.3 all-gather.2
  61.7 48.5 all-gather.4
  258.7 47.1 reduce-scatter.2
  321.2 49.9 reduce-scatter.4

commit v5 on v4

--- a/solution.py
+++ b/solution.py
@@ -18,6 +18,7 @@
 CORES, SIDE = 2, 4
 SIZES = {"core": CORES, "y": SIDE, "z": SIDE, "x": SIDE}
 ORDERS = (("core", "y", "z", "x"), ("core", "z", "y", "x"))
+RELAYED = 1
 NT = (((1,), (1,)), ((), ()))
 NN = (((1,), (0,)), ((), ()))
 
@@ -27,15 +28,15 @@
     return (param - learn_rate * grad / jnp.sqrt(new_state)[:, None], new_state)
 
 
+def shifted(array, by):
+    size = lax.axis_size("bucket")
+    if by == 0:
+        return array
+    return lax.ppermute(array, "bucket", [(i, (i - by) % size) for i in range(size)])
+
+
 def rotate(array, amount):
-    size = lax.axis_size("bucket")
-
-    def move(by):
-        if by == 0:
-            return lambda a: a
-        return lambda a: lax.ppermute(a, "bucket", [(i, (i - by) % size) for i in range(size)])
-
-    return lax.switch(amount, [move(by) for by in range(size)], array)
+    return lax.switch(amount, [lambda a, by=by: shifted(a, by) for by in range(lax.axis_size("bucket"))], array)
 
 
 def split(a):
@@ -206,11 +207,11 @@
 def scatter_right(dst, neg, gy, gn, part_rows, span_len):
     count, width = gy.shape
     span_count, neg_count = neg.shape
-    neg = neg.reshape(-1)
     per = neg_count // span_len
-
-    def kernel(dst, neg, gy_block, gn_block, out, gy, gn, *sums_sem):
-        *sums, sem = sums_sem
+    draws = [neg[:, k * span_len : (k + 1) * span_len].reshape(-1) for k in range(per)]
+
+    def kernel(dst, *rest):
+        draws, (gy_block, gn_block, out, gy, gn, sem), sums = rest[:per], rest[per : per + 6], rest[per + 6 :]
         b = pl.program_id(0)
         edge_sums, neg_sums = sums[:2], sums[2:]
         gy[...] = gy_block[...]
@@ -224,12 +225,12 @@
         @pl.loop(0, span_len // UNROLL)
         def _(i):
             e0 = pl.multiple_of(i * UNROLL, UNROLL)
-            n0 = pl.multiple_of(i * UNROLL * per, UNROLL * per)
+            at = b * span_len + e0
             for s in range(UNROLL):
-                edge_sums[s % 2][pl.ds(dst[b * span_len + e0 + s], 1), :] += gy[pl.ds(e0 + s, 1), :]
+                edge_sums[s % 2][pl.ds(dst[at + s], 1), :] += gy[pl.ds(e0 + s, 1), :]
                 for k in range(per):
-                    m = n0 + per * s + k
-                    neg_sums[(per * s + k) % len(neg_sums)][pl.ds(neg[b * neg_count + m], 1), :] += gn[pl.ds(m, 1), :]
+                    row = draws[k][at + s]
+                    neg_sums[(per * s + k) % len(neg_sums)][pl.ds(row, 1), :] += gn[pl.ds(k * span_len + e0 + s, 1), :]
 
         @pl.when(b == span_count - 1)
         def _():
@@ -244,16 +245,16 @@
         kernel,
         grid=(span_count,),
         out_shape=jax.ShapeDtypeStruct((part_rows, width), jnp.float32),
-        in_specs=[scalars] * 2
+        in_specs=[scalars] * (1 + per)
         + [pl.BlockSpec((span_len, width), lambda b: (b, 0)), pl.BlockSpec((neg_count, width), lambda b: (b, 0))],
         out_specs=pl.BlockSpec(memory_space=pl.ANY),
         scratch_shapes=[pltpu.VMEM((span_len, width), jnp.float32), pltpu.VMEM((neg_count, width), jnp.float32)]
-        + [sums] * (2 + NEG_SUMS)
-        + [pltpu.SemaphoreType.DMA],
+        + [pltpu.SemaphoreType.DMA]
+        + [sums] * (2 + NEG_SUMS),
         compiler_params=params(),
         cost_estimate=pl.CostEstimate(flops=0, bytes_accessed=40 * count * width, transcendentals=0),
         name="scatter_right",
-    )(dst, neg, gy, gn)
+    )(dst, *draws, gy, gn)
 
 
 def split_place(bucket):
@@ -277,7 +278,9 @@
         levels = len(ORDERS[0])
         parts = [scratch[k * levels : (k + 1) * levels] for k in range(len(ORDERS))]
         arrived = [scratch[(len(ORDERS) + k) * levels : (len(ORDERS) + k + 1) * levels] for k in range(len(ORDERS))]
-        send_in, recv_in, send_out, recv_out = scratch[2 * len(ORDERS) * levels :]
+        rest = scratch[2 * len(ORDERS) * levels :]
+        send_in, recv_in, send_out, recv_out, send_on, recv_on = rest[:6]
+        staged = rest[6:]
         place = split_place(lax.axis_index("bucket"))
         barrier = pltpu.get_barrier_semaphore()
         greeted = 0
@@ -297,17 +300,57 @@
                 device_id_type=MESH,
             )
 
+        def pass_on(source, target, k, index, by, axis):
+            return pltpu.make_async_remote_copy(
+                src_ref=source,
+                dst_ref=target,
+                send_sem=send_on.at[k, index],
+                recv_sem=recv_on.at[k, index],
+                device_id=peer_of(place, axis, by),
+                device_id_type=MESH,
+            )
+
         lows = [k * half for k in range(len(ORDERS))]
         starts = [[] for _ in ORDERS]
         for level in range(levels):
             copies = []
+            if level == RELAYED:
+                relays = []
+                for k, order in enumerate(ORDERS):
+                    axis = order[level]
+                    source, slots = parts[k][level - 1], arrived[k][level]
+                    rows = slots.shape[1] // 2
+
+                    def piece(by, upper, axis=axis, rows=rows):
+                        at = lax.rem(place[axis] + by, SIDE) * (2 * rows) + upper * rows
+                        return pl.ds(pl.multiple_of(at, 8), rows)
+
+                    low, high = pl.ds(0, rows), pl.ds(rows, rows)
+                    to_up = pass_on(source.at[piece(2, 0), :], slots.at[2, low, :], k, 0, 1, axis)
+                    to_down = pass_on(source.at[piece(2, 1), :], slots.at[2, high, :], k, 1, SIDE - 1, axis)
+                    plain_up = pass_on(source.at[piece(1, 1), :], slots.at[0, high, :], k, 2, 1, axis)
+                    plain_down = pass_on(source.at[piece(SIDE - 1, 0), :], slots.at[1, low, :], k, 3, SIDE - 1, axis)
+                    for c in (to_up, to_down, plain_up, plain_down):
+                        c.start()
+                    relays.append((k, axis, source, slots, piece, low, high, to_up, to_down))
+                    copies += [plain_up, plain_down]
+                for k, axis, source, slots, piece, low, high, to_up, to_down in relays:
+                    to_up.wait()
+                    staged[k][0] = source[piece(1, 0), :] + slots[2, low, :]
+                    sum_up = pass_on(staged[k].at[0], slots.at[0, low, :], k, 4, 1, axis)
+                    sum_up.start()
+                    to_down.wait()
+                    staged[k][1] = source[piece(SIDE - 1, 1), :] + slots[2, high, :]
+                    sum_down = pass_on(staged[k].at[1], slots.at[1, high, :], k, 5, SIDE - 1, axis)
+                    sum_down.start()
+                    copies += [sum_up, sum_down]
             for k, order in enumerate(ORDERS):
                 axis = order[level]
                 size = SIZES[axis]
                 block = half // math.prod(SIZES[a] for a in order[: level + 1])
                 source = grad if level == 0 else parts[k][level - 1]
                 base = lows[k] if level == 0 else 0
-                for by in range(1, size):
+                for by in range(1, 1 if level == RELAYED else size):
                     other = lax.rem(place[axis] + by, size)
                     c = copy(
                         source.at[pl.ds(pl.multiple_of(base + other * block, 8), block), :],
@@ -325,7 +368,7 @@
                 source = grad if level == 0 else parts[k][level - 1]
                 base = lows[k] if level == 0 else 0
                 own = source[pl.ds(pl.multiple_of(base + place[axis] * block, 8), block), :]
-                for by in range(1, size):
+                for by in range(1, SIDE - 1 if level == RELAYED else size):
                     own = own + arrived[k][level][by - 1]
                 starts[k].append(place[axis] * block)
                 if level < levels - 1:
@@ -335,7 +378,34 @@
                     out[pl.ds(pl.multiple_of(first, 8), block), :] = own
         for level in reversed(range(levels)):
             copies = []
-            for k, order in enumerate(ORDERS):
+            if level == RELAYED:
+                relays = []
+                for k, order in enumerate(ORDERS):
+                    axis = order[level]
+                    block = half // math.prod(SIZES[a] for a in order[: level + 1])
+                    base = lows[k] + sum(starts[k][:level])
+
+                    def piece(by, skip, rows, axis=axis, block=block, base=base):
+                        at = base + lax.rem(place[axis] + by, SIDE) * block + skip
+                        return out.at[pl.ds(pl.multiple_of(at, 8), rows), :]
+
+                    own = piece(0, 0, block)
+                    to_up = pass_on(own, own, k, 6, 1, axis)
+                    to_down = pass_on(own, own, k, 7, SIDE - 1, axis)
+                    to_up.start()
+                    to_down.start()
+                    relays.append((k, axis, block // 2, piece, to_up, to_down))
+                for k, axis, rows, piece, to_up, to_down in relays:
+                    to_up.wait()
+                    below = piece(SIDE - 1, 0, rows)
+                    on_up = pass_on(below, below, k, 8, 1, axis)
+                    on_up.start()
+                    to_down.wait()
+                    above = piece(1, rows, rows)
+                    on_down = pass_on(above, above, k, 9, SIDE - 1, axis)
+                    on_down.start()
+                    copies += [on_up, on_down]
+            for k, order in enumerate(ORDERS if level != RELAYED else ()):
                 axis = order[level]
                 block = half // math.prod(SIZES[a] for a in order[: level + 1])
                 first = lows[k] + sum(starts[k][: level + 1])
@@ -353,6 +423,9 @@
             block = half // math.prod(SIZES[a] for a in order[: level + 1])
             parts.append(pltpu.VMEM((block, width), jnp.float32))
             arrived.append(pltpu.VMEM((SIZES[order[level]] - 1, block, width), jnp.float32))
+    rows = half // math.prod(SIZES[a] for a in ORDERS[0][: RELAYED + 1]) // 2
+    staged = [pltpu.VMEM((2, rows, width), jnp.float32) for _ in ORDERS]
+    on_sems = pltpu.SemaphoreType.DMA((len(ORDERS), 10))
     whole = pl.BlockSpec(memory_space=pltpu.VMEM)
     sems = pltpu.SemaphoreType.DMA((len(ORDERS), len(ORDERS[0]), SIDE))
     return pl.pallas_call(
@@ -360,11 +433,11 @@
         out_shape=jax.ShapeDtypeStruct(grads.shape, jnp.float32),
         in_specs=[whole],
         out_specs=whole,
-        scratch_shapes=parts + arrived + [sems] * 4,
+        scratch_shapes=parts + arrived + [sems] * 4 + [on_sems] * 2 + staged,
         compiler_params=pltpu.CompilerParams(
             collective_id=0, has_side_effects=True, vmem_limit_bytes=40 * 1024 * 1024
         ),
-        cost_estimate=pl.CostEstimate(flops=2 * rows * width, bytes_accessed=40 * rows * width, transcendentals=0),
+        cost_estimate=pl.CostEstimate(flops=2 * half * width, bytes_accessed=80 * half * width, transcendentals=0),
         name="relation_sums",
     )(grads)
 
@@ -396,11 +469,21 @@
     right_grad = scatter_right(targets, negatives, grad_y, grad_n, part_rows, span_len)
     right_grad, left_share = lax.optimization_barrier((right_grad, left_share))
     right_share = lax.psum_scatter(right_grad, "dom", scatter_dimension=0, tiled=True)
-    right_share = rotate(right_share, jnp.mod(-rotation[0], trainers))
-    new_left, new_left_acc = adagrad(left_table, left_state, left_share)
+    rel_total = sum_everywhere(rel_grad)
+
+    def close(by):
+        def branch(right_share, left_share, rel_total):
+            moved = shifted(right_share, by)
+            return moved, adagrad(left_table, left_state, left_share), adagrad(relations, relation_state, rel_total)
+
+        return branch
+
+    backward = jnp.mod(-rotation[0], trainers)
+    right_share, left_new, rel_new = lax.switch(
+        backward, [close(by) for by in range(trainers)], right_share, left_share, rel_total
+    )
     new_right, new_right_acc = adagrad(right_table, right_state, right_share)
-    rel_total = sum_everywhere(rel_grad)
-    new_rel, new_rel_acc = adagrad(relations, relation_state, rel_total)
+    (new_left, new_left_acc), (new_rel, new_rel_acc) = left_new, rel_new
     return (new_left, new_right, new_left_acc, new_right_acc, new_rel, new_rel_acc)
 
 

time: 435 us -> 459 us (1.055); the launches traced: 433 us -> 450 us
  loops' own time: 0.05 us -> 22.5 us
  waiting for transfers between devices: 92.7 us -> 85.6 us
  Pallas kernels: 303 us -> 297 us
    another operation x2, loops' own time: 0.05 us -> 22.5 us  [the longest x1 22.2 us: body(): lax.switch(backward, [close(by) for by in range(trainers)], right_share,...]
    pallas_call x1, Pallas kernels: 62.3 us -> 56.7 us  [scatter_right(): pl.pallas_call(kernel, grid=(span_count,), out_shape=jax.ShapeDtypeStruct...]
    all_gather x1, waiting for transfers between devices: 23.8 us -> 19 us  [body(): left_full = lax.all_gather(left_table, 'dom', axis=0, tiled=True)]
  transfers between devices with their start and end apart: 6 -> 6, of which waited for: 4 -> 4; matrix products, arithmetic and copies ran while one was open for 2% -> 2% of each run, Pallas kernels for 36% -> 33%
where the time goes in v5:
time: 459 us; the launch traced here: 450 us
  Pallas kernels  297 us (65%)
  waiting for transfers between devices  85.6 us (19%)
  loops' own time  22.5 us (5%)
  between operations  15.3 us (3%)
  other arithmetic  14.9 us (3%)
  starting transfers between devices  9 us (2%)
  local copies, waits for them, and re-layouts  5.2 us (1%)
    pallas_call x1, Pallas kernels, score_blocks(): pl.pallas_call(kernel, grid=(span_count + 1,), out_shape=[jax.ShapeDtypeS...  148 us
    pallas_call x1, Pallas kernels, sum_everywhere(): pl.pallas_call(kernel, out_shape=jax.ShapeDtypeStruct(grads.shape, jnp.fl...  60.1 us
    pallas_call x1, Pallas kernels, scatter_right(): pl.pallas_call(kernel, grid=(span_count,), out_shape=jax.ShapeDtypeStruct...  56.7 us
    ppermute x2, waiting for transfers between devices, shifted(): lax.ppermute(array, 'bucket', [(i, (i - by) % size) for i in range(size)])  48 us
    pallas_call x1, Pallas kernels, look_up(): pl.pallas_call(kernel, grid=(count // span_len,), out_shape=[jax.ShapeDty...  32.4 us
    another operation x1, loops' own time, body(): lax.switch(backward, [close(by) for by in range(trainers)], right_share,...  22.2 us
    all_gather x1, waiting for transfers between devices, body(): left_full = lax.all_gather(left_table, 'dom', axis=0, tiled=True)  19 us
    all_gather x1, waiting for transfers between devices, body(): right_full = lax.all_gather(right_rows, 'dom', axis=0, tiled=True)  17.9 us
  transfers between devices with their start and end apart: 6, of which 4 were waited for; matrix products, arithmetic and copies ran while one was open for 2% of the time, Pallas kernels for 33%

profile of v5, /device:TPU:25, one launch (start us, length us, event | category | flops | bytes accessed | tf_op | source)
XLA Modules:
  0.0 449.8 jit_solution(3063642778377427153)
XLA Ops:
  7.2 0.0 all-gather.3.cloned.1.call-start
  7.2 0.7 all-gather.3.cloned.1.call-update
  7.9 0.0 all-gather.5.cloned.1.call-start
  8.6 31.7 %conditional.2 = (f32[2048,128]{1,0:T(8,128)}) conditional(s32[]{:T(128)} %clamp.7, f32[2048,128]{1,0:T(8,128)} %param.76, f32[2048,128]{1,0:T(8,128)} %param.76, f32[2048,128]{1,0:T(8,128)} %param.76, f32[2048,128]{1,0:T(8,128)} %param.76, f32[2048,128]{1,0:T(8,128)} %param.76, f32[2048,128]{1,0:T(8,128)} %param.76, ...), branch_computations={%region_0.1_spmd, %region_1.2_spmd, %region_2.3_spmd, %region_3.4_... | conditional | bytes 4194352 | solution.py:39
  8.7 5.1 %collective-permute-start.12 = (f32[2048,128]{1,0:T(8,128)}, f32[2048,128]{1,0:T(8,128)}, u32[]{:S(2)}, u32[]{:S(2)}) collective-permute-start(f32[2048,128]{1,0:T(8,128)} %param.13), channel_id=1, source_target_pairs={{0,76},{4,80},{8,84},{12,88},{16,92},{20,96},{24,100},{28,104},{32... | collective-permute-start | bytes 3145736 | tf_op jit(solution)/shard_map/cond/branch_13_fun/ppermute | solution.py:35
  13.7 26.4 %collective-permute-done.12 = f32[2048,128]{1,0:T(8,128)} collective-permute-done((f32[2048,128]{1,0:T(8,128)}, f32[2048,128]{1,0:T(8,128)}, u32[]{:S(2)}, u32[]{:S(2)}) %collective-permute-start.12) | collective-permute-done | bytes 1048608 | tf_op jit(solution)/shard_map/cond/branch_13_fun/ppermute | solution.py:35
  40.3 0.0 all-gather.5.cloned.1.call-update
  40.3 0.0 reduce-scatter.3.cloned.1.call-start
  40.4 0.7 copy.19
  41.1 19.0 %all-gather.3.cloned.1.call-done.left = f32[8192,128]{1,0:T(8,128)} async-done(((f32[2048,128]{1,0:T(8,128)}), f32[8192,128]{1,0:T(8,128)}) %all-gather.3.cloned.1.call-update) | async-done | bytes 4194320 | tf_op jit(solution)/shard_map/all_gather | solution.py:459
  60.0 32.4 %look_up.1 = (f32[16384,128]{1,0:T(8,128)}, f32[16384,128]{1,0:T(8,128)}) custom-call(s32[16384]{0:T(1024)} %src.3, s32[16384]{0:T(1024)} %rid.3, f32[8192,128]{1,0:T(8,128)} %all-gather.3.cloned.1.call-done.left, f32[8192,128]{1,0:T(8,128)} %rel.1), custom_call_target="tpu_custom_call" | custom-call | bytes 20971520 | tf_op jit(solution)/shard_map/look_up/pallas_call | solution.py:73
  92.5 17.9 %all-gather.5.cloned.1.call-done.right_hbm = f32[8192,128]{1,0:T(8,128)} async-done(((f32[2048,128]{1,0:T(8,128)}), f32[8192,128]{1,0:T(8,128)}) %all-gather.5.cloned.1.call-update) | async-done | bytes 4194320 | tf_op jit(solution)/shard_map/all_gather | solution.py:461
  110.3 148.1 %score_blocks.1 = (f32[8192,128]{1,0:T(8,128)}, f32[8192,128]{1,0:T(8,128)}, f32[16384,128]{1,0:T(8,128)}, f32[32768,128]{1,0:T(8,128)}) custom-call(s32[16384]{0:T(1024)} %src.3, s32[16384]{0:T(1024)} %dst.3, s32[16384]{0:T(1024)} %rid.3, s32[32768]{0:T(1024)} %bitcast.14, f32[16384,128]{1,0:T(8,128)} %get-tuple-element.756.x, ...), custom_call_target="tpu_custom_call" | custom-call | tf_op jit(solution)/shard_map/score_blocks/pallas_call | solution.py:183
  258.5 0.0 reduce-scatter.5.cloned.1.call-start
  258.6 0.6 copy.17
  259.2 0.6 copy.18
  259.9 56.7 %scatter_right.1 = f32[8192,128]{1,0:T(8,128)} custom-call(s32[16384]{0:T(1024)} %dst.3, s32[16384]{0:T(1024)} %bitcast.15, s32[16384]{0:T(1024)} %bitcast.16, f32[16384,128]{1,0:T(8,128)} %get-tuple-element.758.rest_2_, f32[32768,128]{1,0:T(8,128)} %get-tuple-element.759.rest_3_), custom_call_target="tpu_custom_call" | custom-call | bytes 83886080 | tf_op jit(solution)/shard_map/scatter_right/pallas_call | solution.py:244
  316.6 0.0 reduce-scatter.3.cloned.1.call-done
  316.6 2.2 copy-done
  318.8 60.1 %relation_sums.1 = f32[8192,128]{1,0:T(8,128)} custom-call(f32[8192,128]{1,0:T(8,128)S(1)} %copy-done), custom_call_target="tpu_custom_call" | custom-call | flops 1048576 | bytes 41943040 | tf_op jit(solution)/shard_map/relation_sums/pallas_call | solution.py:431
  378.9 0.0 reduce-scatter.5.cloned.1.call-done
  379.0 57.7 %conditional.3 = (f32[2048,128]{1,0:T(8,128)}, f32[2048,128]{1,0:T(8,128)S(1)}, f32[2048]{0:T(1024)S(1)}, f32[8192,128]{1,0:T(8,128)S(1)}, f32[8192]{0:T(1024)S(1)}) conditional(s32[]{:T(128)} %clamp.6, (f32[2048,128]{1,0:T(8,128)S(1)}, f32[2048]{0:T(1024)S(1)}, f32[2048,128]{1,0:T(8,128)S(1)}, ...), branch_computations={%region_34.37_spmd, %region_37.40_spmd, %region_40.43_spmd, %regio... | conditional | flops 6563840 | bytes 44286060 | solution.py:482
  386.7 3.8 collective-permute-start.49
  390.5 3.3 multiply_reduce_fusion.38
  393.9 5.0 %divide_subtract_fusion.38 = f32[8192,128]{1,0:T(8,128)S(1)} fusion(f32[8192,128]{1,0:T(8,128)} %get-tuple-element.650, f32[8192,128]{1,0:T(8,128)S(1)} %copy-done.20, f32[8192]{0:T(1024)S(1)} %get-tuple-element.845), kind=kLoop, calls=%fused_computation.114 | loop fusion | flops 3145728 | bytes 12615680 | tf_op jit(solution)/shard_map/cond/branch_19_fun/sub | solution.py:28
  398.9 0.3 multiply_reduce_fusion.39
  399.3 0.3 divide_subtract_fusion.39
  399.6 21.6 %collective-permute-done.49 = f32[2048,128]{1,0:T(8,128)S(1)} collective-permute-done((f32[2048,128]{1,0:T(8,128)}, f32[2048,128]{1,0:T(8,128)S(1)}, u32[]{:S(2)}, u32[]{:S(2)}) %collective-permute-start.49) | collective-permute-done | bytes 1048608 | tf_op jit(solution)/shard_map/cond/branch_19_fun/ppermute | solution.py:35
  421.2 1.0 copy.147
  436.7 2.4 multiply_reduce_fusion.64
  439.1 0.6 fusion.64
  439.7 2.9 divide_subtract_fusion.64
  (28 shorter events, 0.1 us)
Async XLA Ops:
  7.2 33.2 %copy-start.39 = (s32[32,1024]{1,0:T(8,128)S(1)}, s32[32,1024]{1,0:T(8,128)}, u32[]{:S(2)}) copy-start(s32[32,1024]{1,0:T(8,128)} %param.82) | copy-start | bytes 393220
  7.2 52.9 %all-gather.3.cloned.1.call-start = ((), (), s32[]{:S(2)}) async-start(), calls=%async_computation.2 | async-start | bytes 5242880 | tf_op jit(solution)/shard_map/all_gather | solution.py:459
  7.9 102.4 %all-gather.5.cloned.1.call-start = ((), (), s32[]{:S(2)}) async-start(), calls=%async_computation.3 | async-start | bytes 5242880 | tf_op jit(solution)/shard_map/all_gather | solution.py:461
  8.7 31.5 %collective-permute-start.12 = (f32[2048,128]{1,0:T(8,128)}, f32[2048,128]{1,0:T(8,128)}, u32[]{:S(2)}, u32[]{:S(2)}) collective-permute-start(f32[2048,128]{1,0:T(8,128)} %param.13), channel_id=1, source_target_pairs={{0,76},{4,80},{8,84},{12,88},{16,92},{20,96},{24,100},{28,104},{32... | collective-permute-start | bytes 3145736 | tf_op jit(solution)/shard_map/cond/branch_13_fun/ppermute | solution.py:35
  40.3 276.2 %reduce-scatter.3.cloned.1.call-start = ((), (), s32[]{:S(2)}) async-start(), calls=%async_computation.4 | async-start | bytes 5242880 | tf_op jit(solution)/shard_map/reduce_scatter | solution.py:468
  258.5 120.4 %reduce-scatter.5.cloned.1.call-start = ((), (), s32[]{:S(2)}) async-start(), calls=%async_computation.5 | async-start | bytes 5242880 | tf_op jit(solution)/shard_map/reduce_scatter | solution.py:471
  316.6 2.2 copy-start
  318.8 60.1 %copy-start.33 = (f32[2048,128]{1,0:T(8,128)S(1)}, f32[2048,128]{1,0:T(8,128)}, u32[]{:S(2)}) copy-start(f32[2048,128]{1,0:T(8,128)} %reduce-scatter.3.cloned.1.call-done) | copy-start | bytes 3145732
  318.8 60.1 %copy-start.34 = (f32[2048,128]{1,0:T(8,128)S(1)}, f32[2048,128]{1,0:T(8,128)}, u32[]{:S(2)}) copy-start(f32[2048,128]{1,0:T(8,128)} %param.75) | copy-start | bytes 3145732
  318.8 60.1 %copy-start.35 = (f32[8192]{0:T(1024)S(1)}, f32[8192]{0:T(1024)}, u32[]{:S(2)}) copy-start(f32[8192]{0:T(1024)} %param.85) | copy-start | bytes 98308
  318.8 60.1 %copy-start.36 = (f32[2048]{0:T(1024)S(1)}, f32[2048]{0:T(1024)}, u32[]{:S(2)}) copy-start(f32[2048]{0:T(1024)} %param.77) | copy-start | bytes 24580
  379.0 60.1 %copy-start.41 = (f32[2048]{0:T(1024)S(1)}, f32[2048]{0:T(1024)}, u32[]{:S(2)}) copy-start(f32[2048]{0:T(1024)} %param.78) | copy-start | bytes 24580
  386.7 7.2 %copy-start.20 = (f32[8192,128]{1,0:T(8,128)S(1)}, f32[8192,128]{1,0:T(8,128)}, u32[]{:S(2)}) copy-start(f32[8192,128]{1,0:T(8,128)} %get-tuple-element.651) | copy-start | bytes 12582916 | tf_op jit(solution)/shard_map/cond
  386.7 34.5 %collective-permute-start.49 = (f32[2048,128]{1,0:T(8,128)}, f32[2048,128]{1,0:T(8,128)S(1)}, u32[]{:S(2)}, u32[]{:S(2)}) collective-permute-start(f32[2048,128]{1,0:T(8,128)} %get-tuple-element.646), channel_id=1, source_target_pairs={{0,52},{4,56},{8,60},{12,64},{16,68},{20,72},{24,76},{28,80},{32,8... | collective-permute-start | bytes 3145736 | tf_op jit(solution)/shard_map/cond/branch_19_fun/ppermute | solution.py:35
  436.7 5.9 %copy-start.37 = (f32[8192,128]{1,0:T(8,128)}, f32[8192,128]{1,0:T(8,128)S(1)}, u32[]{:S(2)}) copy-start(f32[8192,128]{1,0:T(8,128)S(1)} %get-tuple-element.754) | copy-start | bytes 12582916
  436.7 5.9 %copy-start.38 = (f32[2048,128]{1,0:T(8,128)}, f32[2048,128]{1,0:T(8,128)S(1)}, u32[]{:S(2)}) copy-start(f32[2048,128]{1,0:T(8,128)S(1)} %get-tuple-element.750) | copy-start | bytes 3145732
  436.7 5.9 %copy-start.40 = (f32[8192]{0:T(1024)}, f32[8192]{0:T(1024)S(1)}, u32[]{:S(2)}) copy-start(f32[8192]{0:T(1024)S(1)} %get-tuple-element.755) | copy-start | bytes 98308
  436.7 5.9 %copy-start.42 = (f32[2048]{0:T(1024)}, f32[2048]{0:T(1024)S(1)}, u32[]{:S(2)}) copy-start(f32[2048]{0:T(1024)S(1)} %get-tuple-element.752) | copy-start | bytes 24580
Sparse Core Ops, SparseCore 0:
  9.7 50.3 all-gather.2
  61.7 48.5 all-gather.4
  258.6 47.1 reduce-scatter.2
  316.7 49.9 reduce-scatter.4
